TPU v7x, 32 devices: a whole 2x2x4 slice. The times are simulated.
32 devices in a mesh: seq: 8 (over z, y), row: 4 (over x, core).
Axes of the slice: x: 2, y: 2, z: 4, core: 2. Of those that a mesh axis runs over, the one named last changes fastest.
Arguments:
- tokens: bfloat16 [2, 4, 8192, 512], P(None, 'row', 'seq'), may hold values from -6 to 6
- cotangent: float32 [2, 4, 8192, 512], P(None, 'row', 'seq'), may hold values from -6 to 6
- resets: int32 [2, 4, 8], P(None, 'row'), may hold values from 0 to 8191, as said below
- ln_gain: float32 [2, 512], replicated, may hold values from 0.25 to 1.75
- ln_bias: float32 [2, 512], replicated, may hold values from -3 to 3
- in_re: bfloat16 [2, 512, 256], replicated, may hold values from -0.1875 to 0.1875
- in_im: bfloat16 [2, 512, 256], replicated, may hold values from -0.1875 to 0.1875
- nu_log: float32 [2, 256], replicated, as said below
- theta_log: float32 [2, 256], replicated, may hold values from -6.9 to -1.2
- out_re: bfloat16 [2, 256, 512], replicated, may hold values from -0.25 to 0.25
- out_im: bfloat16 [2, 256, 512], replicated, may hold values from -0.25 to 0.25
- skip: float32 [2, 512], replicated, may hold values from -3 to 3
- glu_w: bfloat16 [2, 512, 1024], replicated, may hold values from -0.25 to 0.25
- glu_b: float32 [2, 1024], replicated, may hold values from -3 to 3
Outputs:
- activations: float32 [2, 4, 8192, 512], P(None, 'row', 'seq')
- input_grad: float32 [2, 4, 8192, 512], P(None, 'row', 'seq')
- grad_ln_gain: float32 [2, 512], replicated
- grad_ln_bias: float32 [2, 512], replicated
- grad_in_re: float32 [2, 512, 256], replicated
- grad_in_im: float32 [2, 512, 256], replicated
- grad_nu_log: float32 [2, 256], replicated
- grad_theta_log: float32 [2, 256], replicated
- grad_out_re: float32 [2, 256, 512], replicated
- grad_out_im: float32 [2, 256, 512], replicated
- grad_skip: float32 [2, 512], replicated
- grad_glu_w: float32 [2, 512, 1024], replicated
- grad_glu_b: float32 [2, 1024], replicated
Inputs may be any that keep to these rules, and one draw needn't show every extreme that they name: `resets`: each row's positions rise, may repeat, and the first is 0; some row of every draw has a reset at the final position. exp(nu_log) lies between 0.2 / 8192 and 1 / 30.
All inputs are finite; a program needn't handle non-finite values.
Results may differ from a plain program's by a relative error of at most 0.017.
Values sent between devices are 32-bit elements; how exact they have to be, the bound alone decides.
No kernel may reach another device: no remote copies, remote signals or barrier semaphores. Data moves between devices by JAX's collectives and lax.ppermute only.
A program may use at most 256 MiB of HBM per device.

v0:
```python
import jax
import jax.numpy as jnp
from jax import lax
from jax.sharding import PartitionSpec as P

EPS = 1e-05


def entering(shard, axis, combine, identity, reverse):
    size, index = (lax.axis_size(axis), lax.axis_index(axis))
    everything = jax.tree.map(lambda part: lax.all_gather(part, axis), shard)
    start = jax.tree.map(
        lambda part, zero: jnp.broadcast_to(jnp.asarray(zero, part.dtype), part.shape),
        shard,
        identity,
    )

    def turn(k, before):
        at = size - 1 - k if reverse else k
        reached = at > index if reverse else at < index
        new = combine(before, jax.tree.map(lambda part: part[at], everything))
        return jax.tree.map(lambda a, b: jnp.where(reached, a, b), new, before)

    return lax.fori_loop(0, size, turn, start)


def norm_affine(inputs, scale_row, offset_row):
    centre = jnp.mean(inputs, axis=-1, keepdims=True)
    centred = inputs - centre
    spread = jnp.mean(centred * centred, axis=-1, keepdims=True)
    return centred * lax.rsqrt(spread + EPS) * scale_row + offset_row


def decay_terms(nu_row, theta_row):
    speed = jnp.exp(nu_row)
    radius = jnp.exp(-speed)
    phase = jnp.exp(theta_row)
    return (radius * jnp.cos(phase), radius * jnp.sin(phase), jnp.sqrt(-jnp.expm1(-2.0 * speed)))


def combine(first, second):
    first_ar, first_ai, first_br, first_bi = first
    second_ar, second_ai, second_br, second_bi = second
    return (
        first_ar * second_ar - first_ai * second_ai,
        first_ar * second_ai + first_ai * second_ar,
        second_ar * first_br - second_ai * first_bi + second_br,
        second_ar * first_bi + second_ai * first_br + second_bi,
    )


def complex_times(left_real, left_imag, right_real, right_imag):
    return (
        left_real * right_real - left_imag * right_imag,
        left_real * right_imag + left_imag * right_real,
    )


def glu_tail(gate_pair):
    middle = gate_pair.shape[-1] // 2
    return gate_pair[..., :middle] * jax.nn.sigmoid(gate_pair[..., middle:])


def layer_forward(stream, keep_time, params):
    (
        gain_row,
        bias_row,
        in_real,
        in_imag,
        nu_row,
        theta_row,
        out_real,
        out_imag,
        skip_row,
        glu_matrix,
        glu_offset,
    ) = params
    normed = norm_affine(stream, gain_row, bias_row)
    normed_low = normed.astype(jnp.bfloat16)
    proj_real = jnp.einsum("btd,ds->tbs", normed_low, in_real, preferred_element_type=jnp.float32)
    proj_imag = jnp.einsum("btd,ds->tbs", normed_low, in_imag, preferred_element_type=jnp.float32)
    lam_real, lam_imag, gamma_row = decay_terms(nu_row, theta_row)
    decay_real = keep_time[..., None] * lam_real
    decay_imag = keep_time[..., None] * lam_imag
    prod_real, prod_imag, local_real, local_imag = lax.associative_scan(
        combine, (decay_real, decay_imag, gamma_row * proj_real, gamma_row * proj_imag), axis=0
    )
    unit_row = jnp.ones_like(local_real[0])
    zero_row = jnp.zeros_like(local_real[0])
    carried = entering(
        (prod_real[-1], prod_imag[-1], local_real[-1], local_imag[-1]),
        "seq",
        combine,
        (unit_row, zero_row, zero_row, zero_row),
        False,
    )
    carry_real = carried[2][None]
    carry_imag = carried[3][None]
    extra_real, extra_imag = complex_times(prod_real, prod_imag, carry_real, carry_imag)
    state_real = local_real + extra_real
    state_imag = local_imag + extra_imag
    prev_real = jnp.concatenate([carry_real, state_real[:-1]], axis=0)
    prev_imag = jnp.concatenate([carry_imag, state_imag[:-1]], axis=0)
    state_low_real = state_real.astype(jnp.bfloat16)
    state_low_imag = state_imag.astype(jnp.bfloat16)
    mixed = (
        jnp.einsum("tbs,sd->btd", state_low_real, out_real, preferred_element_type=jnp.float32)
        - jnp.einsum("tbs,sd->btd", state_low_imag, out_imag, preferred_element_type=jnp.float32)
        + skip_row * normed
    )
    activated = jax.nn.gelu(mixed).astype(jnp.bfloat16)
    gate_pair = (
        jnp.einsum("btd,de->bte", activated, glu_matrix, preferred_element_type=jnp.float32)
        + glu_offset
    )
    saved = (
        stream,
        normed,
        normed_low,
        proj_real,
        proj_imag,
        decay_real,
        decay_imag,
        prev_real,
        prev_imag,
        state_low_real,
        state_low_imag,
        mixed,
        activated,
        gate_pair,
    )
    return (stream + glu_tail(gate_pair), saved)


def layer_backward(upstream, keep_time, params, saved):
    (
        gain_row,
        bias_row,
        in_real,
        in_imag,
        nu_row,
        theta_row,
        out_real,
        out_imag,
        skip_row,
        glu_matrix,
        glu_offset,
    ) = params
    (
        stream,
        normed,
        normed_low,
        proj_real,
        proj_imag,
        decay_real,
        decay_imag,
        prev_real,
        prev_imag,
        state_low_real,
        state_low_imag,
        mixed,
        activated,
        gate_pair,
    ) = saved
    f32 = jnp.float32
    tail_value, tail_pull = jax.vjp(glu_tail, gate_pair)
    pair_low = tail_pull(upstream)[0].astype(jnp.bfloat16)
    grad_glu = jnp.einsum("btd,bte->de", activated, pair_low, preferred_element_type=f32)
    grad_offset = jnp.sum(pair_low.astype(f32), axis=(0, 1))
    act_grad = jnp.einsum("bte,de->btd", pair_low, glu_matrix, preferred_element_type=f32)
    gelu_value, gelu_pull = jax.vjp(jax.nn.gelu, mixed)
    mixed_low = gelu_pull(act_grad)[0].astype(jnp.bfloat16)
    mixed_wide = mixed_low.astype(f32)
    grad_out_real = jnp.einsum("tbs,btd->sd", state_low_real, mixed_low, preferred_element_type=f32)
    grad_out_imag = -jnp.einsum(
        "tbs,btd->sd", state_low_imag, mixed_low, preferred_element_type=f32
    )
    grad_skip = jnp.sum(mixed_wide * normed, axis=(0, 1))
    adj_real = jnp.einsum("btd,sd->tbs", mixed_low, out_real, preferred_element_type=f32)
    adj_imag = -jnp.einsum("btd,sd->tbs", mixed_low, out_imag, preferred_element_type=f32)
    next_real = jnp.concatenate([decay_real[1:], jnp.ones_like(decay_real[:1])], axis=0)
    next_imag = jnp.concatenate([-decay_imag[1:], jnp.zeros_like(decay_imag[:1])], axis=0)
    back_real, back_imag, loc_real, loc_imag = lax.associative_scan(
        combine, (next_real, next_imag, adj_real, adj_imag), reverse=True, axis=0
    )
    head_real = decay_real[0]
    head_imag = -decay_imag[0]
    span_real, span_imag = complex_times(head_real, head_imag, back_real[0], back_imag[0])
    sent_real, sent_imag = complex_times(head_real, head_imag, loc_real[0], loc_imag[0])
    unit_row = jnp.ones_like(span_real)
    zero_row = jnp.zeros_like(span_real)
    incoming = entering(
        (span_real, span_imag, sent_real, sent_imag),
        "seq",
        combine,
        (unit_row, zero_row, zero_row, zero_row),
        True,
    )
    arrive_real = incoming[2][None]
    arrive_imag = incoming[3][None]
    extra_real, extra_imag = complex_times(back_real, back_imag, arrive_real, arrive_imag)
    total_real = loc_real + extra_real
    total_imag = loc_imag + extra_imag
    keep_cols = keep_time[..., None]
    grad_lam_real = jnp.sum(
        keep_cols * (total_real * prev_real + total_imag * prev_imag), axis=(0, 1)
    )
    grad_lam_imag = jnp.sum(
        keep_cols * (total_imag * prev_real - total_real * prev_imag), axis=(0, 1)
    )
    grad_gamma = jnp.sum(total_real * proj_real + total_imag * proj_imag, axis=(0, 1))
    decay_value, decay_pull = jax.vjp(decay_terms, nu_row, theta_row)
    gamma_row = decay_value[2]
    grad_nu, grad_theta = decay_pull((grad_lam_real, grad_lam_imag, grad_gamma))
    drive_real = (gamma_row * total_real).astype(jnp.bfloat16)
    drive_imag = (gamma_row * total_imag).astype(jnp.bfloat16)
    grad_in_real = jnp.einsum("btd,tbs->ds", normed_low, drive_real, preferred_element_type=f32)
    grad_in_imag = jnp.einsum("btd,tbs->ds", normed_low, drive_imag, preferred_element_type=f32)
    normed_grad = (
        jnp.einsum("tbs,ds->btd", drive_real, in_real, preferred_element_type=f32)
        + jnp.einsum("tbs,ds->btd", drive_imag, in_imag, preferred_element_type=f32)
        + skip_row * mixed_wide
    )
    norm_value, norm_pull = jax.vjp(norm_affine, stream, gain_row, bias_row)
    stream_grad, grad_gain, grad_bias = norm_pull(normed_grad)
    layer_grads = (
        grad_gain,
        grad_bias,
        grad_in_real,
        grad_in_imag,
        grad_nu,
        grad_theta,
        grad_out_real,
        grad_out_imag,
        grad_skip,
        grad_glu,
        grad_offset,
    )
    return (upstream + stream_grad, layer_grads)


def run_rows(tokens, cotangent, keep_mask, weight_set):
    depth = weight_set[0].shape[0]
    keep_time = jnp.swapaxes(keep_mask, 0, 1)
    stream = tokens.astype(jnp.float32)
    kept_layers = []
    for layer_no in range(depth):
        params = tuple((member[layer_no] for member in weight_set))
        stream, saved = layer_forward(stream, keep_time, params)
        kept_layers.append((params, saved))
    upstream = cotangent
    per_layer = [None] * depth
    for layer_no in range(depth - 1, -1, -1):
        params, saved = kept_layers[layer_no]
        upstream, layer_grads = layer_backward(upstream, keep_time, params, saved)
        per_layer[layer_no] = layer_grads
    stacked = tuple(
        (
            jnp.stack([grads_one[slot_no] for grads_one in per_layer])
            for slot_no in range(len(per_layer[0]))
        )
    )
    return (stream, upstream, stacked)


def shards(
    tokens,
    cotangent,
    resets,
    ln_gain,
    ln_bias,
    in_re,
    in_im,
    nu_log,
    theta_log,
    out_re,
    out_im,
    skip,
    glu_w,
    glu_b,
):
    micro, rows_here, length, width = tokens.shape
    positions = lax.axis_index("seq") * length + jnp.arange(length, dtype=jnp.int32)
    reset_hits = jnp.any(resets[:, :, None, :] == positions[None, None, :, None], axis=-1)
    keep_mask = jnp.where(reset_hits, 0.0, 1.0).astype(jnp.float32)
    weight_set = (
        ln_gain,
        ln_bias,
        in_re,
        in_im,
        nu_log,
        theta_log,
        out_re,
        out_im,
        skip,
        glu_w,
        glu_b,
    )
    results = [
        run_rows(tokens[micro_no], cotangent[micro_no], keep_mask[micro_no], weight_set)
        for micro_no in range(micro)
    ]
    activations = jnp.stack([outcome[0] for outcome in results])
    input_grad = jnp.stack([outcome[1] for outcome in results])
    grads = tuple(
        (sum((outcome[2][slot_no] for outcome in results)) for slot_no in range(len(weight_set)))
    )
    (
        grad_gain,
        grad_bias,
        grad_in_real,
        grad_in_imag,
        grad_nu,
        grad_theta,
        grad_out_real,
        grad_out_imag,
        grad_skip,
        grad_glu,
        grad_offset,
    ) = grads
    summed = lax.psum(
        (
            grad_gain,
            grad_bias,
            grad_in_real,
            grad_in_imag,
            grad_nu,
            grad_theta,
            grad_out_real,
            grad_out_imag,
            grad_skip,
            grad_glu,
            grad_offset,
        ),
        ("seq", "row"),
    )
    return (activations, input_grad) + tuple(summed)


def solution(mesh):
    in_specs = (
        P(None, "row", "seq", None),
        P(None, "row", "seq", None),
        P(None, "row", None),
        P(),
        P(),
        P(),
        P(),
        P(),
        P(),
        P(),
        P(),
        P(),
        P(),
        P(),
    )
    out_specs = (
        P(None, "row", "seq", None),
        P(None, "row", "seq", None),
        P(),
        P(),
        P(),
        P(),
        P(),
        P(),
        P(),
        P(),
        P(),
        P(),
        P(),
    )
    return jax.shard_map(shards, mesh=mesh, in_specs=in_specs, out_specs=out_specs, check_vma=False)
```

profile of v0, /device:TPU:0, one launch (start us, length us, event | category | flops | bytes accessed | tf_op | source)
XLA Modules:
  0.0 3660.1 jit_solution(3970110455965007940)
XLA Ops:
  1390.5 23.3 all_gather.122
  1415.9 17.3 all_gather.123
  1472.6 18.3 all_gather.114
  1493.1 16.3 all_gather.115
  1516.8 18.3 all_gather.120
  1542.3 16.3 all_gather.121
  1558.6 5.6 while.138
  1571.6 18.3 all_gather.112
  1597.3 16.3 all_gather.113
  2048.0 18.2 all_gather.124
  2071.6 16.3 all_gather.125
  2100.1 18.7 all_gather.126
  2124.1 16.3 all_gather.127
  2283.1 18.2 all_gather.116
  2306.7 16.3 all_gather.117
  2334.9 18.2 all_gather.118
  2358.5 16.5 all_gather.119
  2398.1 5.8 fusion.79
  2745.8 8.9 rev.73
  2759.8 18.4 all_gather.137
  2778.2 16.3 all_gather.136
  2794.5 8.9 rev.72
  2808.5 18.2 all_gather.139
  2826.8 16.3 all_gather.138
  2843.4 5.9 multiply_reduce_fusion.7
  2852.5 8.9 rev.65
  2861.4 8.9 rev.66
  2870.3 18.2 all_gather.129
  2888.5 16.3 all_gather.128
  2904.9 8.9 rev.64
  2913.7 8.9 rev.67
  2922.6 18.2 all_gather.131
  2940.9 16.3 all_gather.130
  3239.6 8.9 rev.77
  3253.6 18.2 all_gather.141
  3271.9 16.3 all_gather.140
  3288.2 8.9 rev.69
  3302.3 18.2 all_gather.133
  3320.5 16.3 all_gather.132
  3336.8 8.9 rev.76
  3350.9 18.2 all_gather.143
  3369.1 16.3 all_gather.142
  3393.8 8.9 rev.68
  3402.8 8.9 rev.71
  3411.6 18.2 all_gather.135
  3429.9 16.3 all_gather.134
  3484.5 40.4 %all-reduce.664 = (f32[2,512]{1,0:T(2,128)}, f32[2,512]{1,0:T(2,128)}, f32[2,256]{1,0:T(2,128)}, f32[2,256]{1,0:T(2,128)}, f32[2,512]{1,0:T(2,128)}, /*index=5*/f32[2,1024]{1,0:T(2,128)}) all-reduce(f32[2,512]{1,0:T(2,128)S(1)} %maximum_add_fusion.6, ...), channel_id=1, replica_groups=mesh['seq'=8,'row'=4] {'seq','row'}, use_global_device_ids=true, to_apply=%region_37.38 | all-reduce | flops 6144 | bytes 49152 | tf_op jit(solution)/shard_map/psum | solution.py:321
  3535.5 110.0 %all-reduce.668.cloned.1.call-done = (f32[2,512,256]{2,1,0:T(8,128)}, f32[2,512,256]{2,1,0:T(8,128)}, f32[2,256,512]{2,1,0:T(8,128)}, f32[2,256,512]{2,1,0:T(8,128)}, f32[2,512,1024]{2,1,0:T(8,128)}) async-done(((f32[2,512,256]{2,1,0:T(8,128)}, f32[2,512,256]{2,1,0:T(8,128)}, f32[2,256,512]{2,1,0:T(8,128)}, f32[2,256,512]{2,1,0:T(8,128)}, f32[2,512,1024]{2,1,0:T(8,128)}), (f32[2,512,256]{2,1,0:T(8,128)}, ...) | async-done | bytes 8388624 | tf_op jit(solution)/shard_map/psum | solution.py:321
  (4536 shorter events, 2815.0 us)
Async XLA Ops:
  7.2 3638.3 %all-reduce.668.cloned.1.call-start = ((), (), s32[]{:S(2)}) async-start(), calls=%async_computation | async-start | bytes 16777216 | tf_op jit(solution)/shard_map/psum | solution.py:321
  55.5 879.7 %copy-start.44 = (f32[1024,1,256]{2,0,1:T(8,128)}, f32[1024,1,256]{2,0,1:T(8,128)S(1)}, u32[]{:S(2)}) copy-start(f32[1024,1,256]{2,0,1:T(8,128)S(1)} %get-tuple-element.2664) | copy-start | bytes 3145732
  55.5 1089.4 %copy-start.42 = (f32[1024,1,256]{2,0,1:T(8,128)}, f32[1024,1,256]{2,0,1:T(8,128)S(1)}, u32[]{:S(2)}) copy-start(f32[1024,1,256]{2,0,1:T(8,128)S(1)} %get-tuple-element.2666) | copy-start | bytes 3145732
  55.6 1089.4 %copy-start.43 = (f32[1024,1,256]{2,0,1:T(8,128)}, f32[1024,1,256]{2,0,1:T(8,128)S(1)}, u32[]{:S(2)}) copy-start(f32[1024,1,256]{2,0,1:T(8,128)S(1)} %get-tuple-element.2667) | copy-start | bytes 3145732
  383.2 205.2 %copy-start.258 = (f32[255,1,256]{2,0,1:T(8,128)}, f32[255,1,256]{2,0,1:T(8,128)S(1)}, u32[]{:S(2)}) copy-start(f32[255,1,256]{2,0,1:T(8,128)S(1)} %slice.6324) | copy-start | bytes 783364
  400.5 174.1 %copy-start.353 = (f32[127,1,256]{2,0,1:T(8,128)}, f32[127,1,256]{2,0,1:T(8,128)S(1)}, u32[]{:S(2)}) copy-start(f32[127,1,256]{2,0,1:T(8,128)S(1)} %slice.6335) | copy-start | bytes 390148
  439.4 108.4 %copy-start.481 = (f32[15,1,256]{2,0,1:T(8,128)}, f32[15,1,256]{2,0,1:T(8,128)S(1)}, u32[]{:S(2)}) copy-start(f32[15,1,256]{2,0,1:T(8,128)S(1)} %slice.6365) | copy-start | bytes 46084
  686.9 204.9 %copy-start.257 = (f32[255,1,256]{2,0,1:T(8,128)}, f32[255,1,256]{2,0,1:T(8,128)S(1)}, u32[]{:S(2)}) copy-start(f32[255,1,256]{2,0,1:T(8,128)S(1)} %slice.6528) | copy-start | bytes 783364
  704.1 173.8 %copy-start.350 = (f32[127,1,256]{2,0,1:T(8,128)}, f32[127,1,256]{2,0,1:T(8,128)S(1)}, u32[]{:S(2)}) copy-start(f32[127,1,256]{2,0,1:T(8,128)S(1)} %slice.6539) | copy-start | bytes 390148
  742.8 108.3 %copy-start.478 = (f32[15,1,256]{2,0,1:T(8,128)}, f32[15,1,256]{2,0,1:T(8,128)S(1)}, u32[]{:S(2)}) copy-start(f32[15,1,256]{2,0,1:T(8,128)S(1)} %slice.6569) | copy-start | bytes 46084
  974.8 133.8 %copy-start.254 = (f32[255,1,256]{2,0,1:T(8,128)}, f32[255,1,256]{2,0,1:T(8,128)S(1)}, u32[]{:S(2)}) copy-start(f32[255,1,256]{2,0,1:T(8,128)S(1)} %slice.6119) | copy-start | bytes 783364
  984.9 109.7 %copy-start.347 = (f32[127,1,256]{2,0,1:T(8,128)}, f32[127,1,256]{2,0,1:T(8,128)S(1)}, u32[]{:S(2)}) copy-start(f32[127,1,256]{2,0,1:T(8,128)S(1)} %slice.6130) | copy-start | bytes 390148
  993.9 73.9 %copy-start.475 = (f32[15,1,256]{2,0,1:T(8,128)}, f32[15,1,256]{2,0,1:T(8,128)S(1)}, u32[]{:S(2)}) copy-start(f32[15,1,256]{2,0,1:T(8,128)S(1)} %slice.6160) | copy-start | bytes 46084
  1005.0 122.0 %copy-start.109 = (f32[511,1,256]{2,0,1:T(8,128)}, f32[511,1,256]{2,0,1:T(8,128)S(1)}, u32[]{:S(2)}) copy-start(f32[511,1,256]{2,0,1:T(8,128)S(1)} %slice.6102) | copy-start | bytes 1569796
  1008.8 118.1 %copy-start.111 = (f32[511,1,256]{2,0,1:T(8,128)}, f32[511,1,256]{2,0,1:T(8,128)S(1)}, u32[]{:S(2)}) copy-start(f32[511,1,256]{2,0,1:T(8,128)S(1)} %slice.6254) | copy-start | bytes 1569796
  1182.7 134.6 %copy-start.260 = (f32[255,1,256]{2,0,1:T(8,128)}, f32[255,1,256]{2,0,1:T(8,128)S(1)}, u32[]{:S(2)}) copy-start(f32[255,1,256]{2,0,1:T(8,128)S(1)} %slice.5915) | copy-start | bytes 783364
  1193.0 110.4 %copy-start.356 = (f32[127,1,256]{2,0,1:T(8,128)}, f32[127,1,256]{2,0,1:T(8,128)S(1)}, u32[]{:S(2)}) copy-start(f32[127,1,256]{2,0,1:T(8,128)S(1)} %slice.5926) | copy-start | bytes 390148
  1202.5 74.0 %copy-start.484 = (f32[15,1,256]{2,0,1:T(8,128)}, f32[15,1,256]{2,0,1:T(8,128)S(1)}, u32[]{:S(2)}) copy-start(f32[15,1,256]{2,0,1:T(8,128)S(1)} %slice.5956) | copy-start | bytes 46084
  1213.8 122.0 %copy-start.125 = (f32[511,1,256]{2,0,1:T(8,128)}, f32[511,1,256]{2,0,1:T(8,128)S(1)}, u32[]{:S(2)}) copy-start(f32[511,1,256]{2,0,1:T(8,128)S(1)} %slice.6050) | copy-start | bytes 1569796
  1217.6 118.1 %copy-start.127 = (f32[511,1,256]{2,0,1:T(8,128)}, f32[511,1,256]{2,0,1:T(8,128)S(1)}, u32[]{:S(2)}) copy-start(f32[511,1,256]{2,0,1:T(8,128)S(1)} %slice.5898) | copy-start | bytes 1569796
  1387.9 50.1 %copy-start.198 = (f32[1024,1,256]{2,0,1:T(8,128)}, f32[1024,1,256]{2,0,1:T(8,128)S(1)}, u32[]{:S(2)}) copy-start(f32[1024,1,256]{2,0,1:T(8,128)S(1)} %pad.2230) | copy-start | bytes 3145732
  1387.9 50.6 %copy-start.486 = (f32[15,1,256]{2,0,1:T(8,128)S(1)}, f32[15,1,256]{2,0,1:T(8,128)}, u32[]{:S(2)}) copy-start(f32[15,1,256]{2,0,1:T(8,128)} %slice.5150) | copy-start | bytes 46084
  1388.0 50.6 %copy-start.487 = (f32[15,1,256]{2,0,1:T(8,128)S(1)}, f32[15,1,256]{2,0,1:T(8,128)}, u32[]{:S(2)}) copy-start(f32[15,1,256]{2,0,1:T(8,128)} %slice.5213) | copy-start | bytes 46084
  1390.4 54.9 %copy-start.199 = (f32[1024,1,256]{2,0,1:T(8,128)}, f32[1024,1,256]{2,0,1:T(8,128)S(1)}, u32[]{:S(2)}) copy-start(f32[1024,1,256]{2,0,1:T(8,128)S(1)} %pad.2189) | copy-start | bytes 3145732
  1390.4 54.0 %copy-start.452 = (f32[31,1,256]{2,0,1:T(8,128)S(1)}, f32[31,1,256]{2,0,1:T(8,128)}, u32[]{:S(2)}) copy-start(f32[31,1,256]{2,0,1:T(8,128)} %slice.5219) | copy-start | bytes 95236
  1390.4 54.0 %copy-start.453 = (f32[31,1,256]{2,0,1:T(8,128)S(1)}, f32[31,1,256]{2,0,1:T(8,128)}, u32[]{:S(2)}) copy-start(f32[31,1,256]{2,0,1:T(8,128)} %slice.5140) | copy-start | bytes 95236
  1390.4 54.0 %copy-start.501 = (f32[31,1,256]{2,0,1:T(8,128)S(1)}, f32[31,1,256]{2,0,1:T(8,128)}, u32[]{:S(2)}) copy-start(f32[31,1,256]{2,0,1:T(8,128)} %slice.5227) | copy-start | bytes 95236
  1511.3 53.0 %copy-start.679 = (f32[1,1,256]{2,0,1:T(1,128)S(1)}, f32[1,1,256]{2,0,1:T(1,128)}, u32[]{:S(2)}) copy-start(f32[1,1,256]{2,0,1:T(1,128)} %get-tuple-element.2011) | copy-start | bytes 3076
  1537.0 52.9 %copy-start.678 = (f32[1,1,256]{2,0,1:T(1,128)S(1)}, f32[1,1,256]{2,0,1:T(1,128)}, u32[]{:S(2)}) copy-start(f32[1,1,256]{2,0,1:T(1,128)} %get-tuple-element.2012) | copy-start | bytes 3076
  2037.9 50.0 %copy-start.721 = (f32[1,1,256]{2,0,1:T(1,128)S(1)}, f32[1,1,256]{2,0,1:T(1,128)}, u32[]{:S(2)}) copy-start(f32[1,1,256]{2,0,1:T(1,128)} %slice.7237) | copy-start | bytes 3076
  2089.8 50.6 %copy-start.570 = (f32[1,256]{1,0:T(1,128)S(1)}, f32[1,256]{1,0:T(1,128)}, u32[]{:S(2)}) copy-start(f32[1,256]{1,0:T(1,128)} %custom-call.7) | copy-start | bytes 3076
  2089.8 50.6 %copy-start.574 = (f32[1,256]{1,0:T(1,128)S(1)}, f32[1,256]{1,0:T(1,128)}, u32[]{:S(2)}) copy-start(f32[1,256]{1,0:T(1,128)} %custom-call.6) | copy-start | bytes 3076
  2099.4 54.4 %copy-start.456 = (f32[31,1,256]{2,0,1:T(8,128)S(1)}, f32[31,1,256]{2,0,1:T(8,128)}, u32[]{:S(2)}) copy-start(f32[31,1,256]{2,0,1:T(8,128)} %slice.5424) | copy-start | bytes 95236
  2099.4 54.4 %copy-start.457 = (f32[31,1,256]{2,0,1:T(8,128)S(1)}, f32[31,1,256]{2,0,1:T(8,128)}, u32[]{:S(2)}) copy-start(f32[31,1,256]{2,0,1:T(8,128)} %slice.5345) | copy-start | bytes 95236
  2324.9 50.1 %copy-start.564 = (f32[1,256]{1,0:T(1,128)S(1)}, f32[1,256]{1,0:T(1,128)}, u32[]{:S(2)}) copy-start(f32[1,256]{1,0:T(1,128)} %custom-call.3) | copy-start | bytes 3076
  2324.9 50.1 %copy-start.567 = (f32[1,256]{1,0:T(1,128)S(1)}, f32[1,256]{1,0:T(1,128)}, u32[]{:S(2)}) copy-start(f32[1,256]{1,0:T(1,128)} %custom-call.2) | copy-start | bytes 3076
  2403.9 208.3 %copy-start.18 = (bf16[1,1024,512]{2,1,0:T(8,128)(2,1)}, bf16[1,1024,512]{2,1,0:T(8,128)(2,1)S(1)}, u32[]{:S(2)}) copy-start(bf16[1,1024,512]{2,1,0:T(8,128)(2,1)S(1)} %fusion.79) | copy-start | bytes 3145732
  2904.8 52.3 %copy-start.616 = (f32[1,256]{1,0:T(1,128)S(1)}, f32[1,256]{1,0:T(1,128)}, u32[]{:S(2)}) copy-start(f32[1,256]{1,0:T(1,128)} %custom-call.9) | copy-start | bytes 3076
  2904.8 52.3 %copy-start.617 = (f32[1,256]{1,0:T(1,128)S(1)}, f32[1,256]{1,0:T(1,128)}, u32[]{:S(2)}) copy-start(f32[1,256]{1,0:T(1,128)} %custom-call.8) | copy-start | bytes 3076
  2904.8 52.8 %copy-start.538 = (f32[1,1024]{1,0:T(1,128)S(1)}, f32[1,1024]{1,0:T(1,128)}, u32[]{:S(2)}) copy-start(f32[1,1024]{1,0:T(1,128)} %copy-done.537) | copy-start | bytes 12292
  2904.8 52.8 %copy-start.566 = (f32[1,256]{1,0:T(1,128)S(1)}, f32[1,256]{1,0:T(1,128)}, u32[]{:S(2)}) copy-start(f32[1,256]{1,0:T(1,128)} %copy-done.565) | copy-start | bytes 3076
  2904.8 52.8 %copy-start.569 = (f32[1,256]{1,0:T(1,128)S(1)}, f32[1,256]{1,0:T(1,128)}, u32[]{:S(2)}) copy-start(f32[1,256]{1,0:T(1,128)} %copy-done.568) | copy-start | bytes 3076
  2986.5 175.3 %copy-start.6 = (bf16[1,1024,512]{2,1,0:T(8,128)(2,1)}, bf16[1,1024,512]{2,1,0:T(8,128)(2,1)S(1)}, u32[]{:S(2)}) copy-start(bf16[1,1024,512]{2,1,0:T(8,128)(2,1)S(1)} %fusion.58) | copy-start | bytes 3145732
  3393.8 52.3 %copy-start.612 = (f32[1,256]{1,0:T(1,128)S(1)}, f32[1,256]{1,0:T(1,128)}, u32[]{:S(2)}) copy-start(f32[1,256]{1,0:T(1,128)} %custom-call.11) | copy-start | bytes 3076
  3393.8 52.3 %copy-start.613 = (f32[1,256]{1,0:T(1,128)S(1)}, f32[1,256]{1,0:T(1,128)}, u32[]{:S(2)}) copy-start(f32[1,256]{1,0:T(1,128)} %custom-call.10) | copy-start | bytes 3076
  3393.8 52.9 %copy-start.539 = (f32[1,1024]{1,0:T(1,128)S(1)}, f32[1,1024]{1,0:T(1,128)}, u32[]{:S(2)}) copy-start(f32[1,1024]{1,0:T(1,128)} %copy-done.537) | copy-start | bytes 12292
  3393.8 52.9 %copy-start.580 = (f32[1,256]{1,0:T(1,128)S(1)}, f32[1,256]{1,0:T(1,128)}, u32[]{:S(2)}) copy-start(f32[1,256]{1,0:T(1,128)} %copy-done.579) | copy-start | bytes 3076
  3393.8 52.9 %copy-start.583 = (f32[1,256]{1,0:T(1,128)S(1)}, f32[1,256]{1,0:T(1,128)}, u32[]{:S(2)}) copy-start(f32[1,256]{1,0:T(1,128)} %copy-done.582) | copy-start | bytes 3076
  (812 other events, 8166.2 us)
Sparse Core Ops, SparseCore 0:
  3465.1 180.3 all-reduce.667
where the time goes:
time: 3730 us; the launch traced here: 3660 us
  local copies, waits for them, and re-layouts  2090 us (56%)
  other arithmetic  747 us (20%)
  blocking collectives  600 us (16%)
  waiting for transfers between devices  110 us (3%)
  matrix products  80.8 us (2%)
    slice x584, local copies, waits for them, and re-layouts, layer_backward(): lax.associative_scan(combine, (next_real, next_imag, adj_real, adj_imag),...  688 us
    all_gather x32, blocking collectives, entering(): everything = jax.tree.map(lambda part: lax.all_gather(part, axis), shard)  559 us
    slice x548, local copies, waits for them, and re-layouts, layer_forward(): lax.associative_scan(combine, (decay_real, decay_imag, gamma_row * proj_r...  497 us
    pad x288, local copies, waits for them, and re-layouts, layer_backward(): lax.associative_scan(combine, (next_real, next_imag, adj_real, adj_imag),...  426 us
    pad x288, local copies, waits for them, and re-layouts, layer_forward(): lax.associative_scan(combine, (decay_real, decay_imag, gamma_row * proj_r...  245 us
    add x156, other arithmetic, layer_backward(): lax.associative_scan(combine, (next_real, next_imag, adj_real, adj_imag),...  163 us
    rev x16, local copies, waits for them, and re-layouts, layer_backward(): lax.associative_scan(combine, (next_real, next_imag, adj_real, adj_imag),...  123 us
    psum x1, waiting for transfers between devices, shards(): lax.psum((grad_gain, grad_bias, grad_in_real, grad_in_imag, grad_nu, grad...  110 us

commit v1 on v0

v1 whole, which is shorter than its diff:
```python
import functools

import jax
import jax.numpy as jnp
from jax import lax
from jax.experimental import pallas as pl
from jax.experimental.pallas import tpu as pltpu
from jax.sharding import PartitionSpec as P

EPS = 1e-05
CHUNKS = 8
LANES = 128
VMEM_LIMIT = 56 << 20
F32 = jnp.float32
BF16 = jnp.bfloat16
GELU_C = 0.7978845608028654
GELU_A = 0.044715


def dot(left, right):
    return jnp.dot(left, right, preferred_element_type=F32)


def dot_right_t(left, right):
    return lax.dot_general(left, right, (((1,), (1,)), ((), ())), preferred_element_type=F32)


def dot_left_t(left, right):
    return lax.dot_general(left, right, (((0,), (0,)), ((), ())), preferred_element_type=F32)


def normalize(inputs):
    centre = jnp.mean(inputs, axis=-1, keepdims=True)
    centred = inputs - centre
    spread = jnp.mean(centred * centred, axis=-1, keepdims=True)
    scale = lax.rsqrt(spread + EPS)
    return centred * scale, scale


def sigmoid(gate):
    return 0.5 * jnp.tanh(0.5 * gate) + 0.5


def gelu_tanh(mixed):
    return jnp.tanh(GELU_C * (mixed + GELU_A * mixed * mixed * mixed))


def gelu_slope(mixed, bend):
    inner = GELU_C * (1.0 + (3.0 * GELU_A) * mixed * mixed)
    return 0.5 * (1.0 + bend) + 0.5 * mixed * (1.0 - bend * bend) * inner


def times(left, right):
    return (
        left[0] * right[0] - left[1] * right[1],
        left[0] * right[1] + left[1] * right[0],
    )


def to_steps(block):
    return jnp.swapaxes(block, 0, 1).reshape(-1, block.shape[-1])


def from_steps(rows, group):
    return jnp.swapaxes(rows.reshape(-1, group, rows.shape[-1]), 0, 1)


def wide(keep, states):
    return jnp.concatenate([keep] * (states // LANES), axis=1)


def split(value):
    half = value.shape[-1] // 2
    return value[:, :half], value[:, half:]


def spread_row(row, count):
    return jnp.broadcast_to(row, (count, row.shape[-1]))


def rows_of(step, group):
    return slice(step * group, (step + 1) * group)


def scan_up(drive_ref, keep_ref, lam, state, steps, group, store_ref=None):
    states = lam[0].shape[-1]
    for step in range(steps):
        rows = rows_of(step, group)
        keep = wide(keep_ref[rows, :], states)
        turned = times(lam, state)
        state = (
            keep * turned[0] + drive_ref[rows, :states],
            keep * turned[1] + drive_ref[rows, states:],
        )
        if store_ref is not None:
            store_ref[rows, :states] = state[0]
            store_ref[rows, states:] = state[1]
    return state


def chunk_totals(factor, value, count, reverse):
    pieces = []
    for seq_no in range(count):
        rows = rows_of(seq_no, CHUNKS)
        a = (factor[0][rows], factor[1][rows])
        x = (value[0][rows], value[1][rows])
        place = lax.broadcasted_iota(jnp.int32, a[0].shape, 0)
        shift = 1
        while shift < CHUNKS:
            turn = CHUNKS - shift if reverse else shift
            valid = place < CHUNKS - shift if reverse else place >= shift
            a_before = tuple(pltpu.roll(part, turn, 0) for part in a)
            x_before = tuple(pltpu.roll(part, turn, 0) for part in x)
            a_new = times(a_before, a)
            x_new = times(a, x_before)
            x = tuple(jnp.where(valid, new + old, old) for new, old in zip(x_new, x))
            a = tuple(jnp.where(valid, new, old) for new, old in zip(a_new, a))
            shift *= 2
        pieces.append((a, x))
    return pieces


def write_totals(pieces, pre_ref, end_ref, reverse):
    count = len(pieces)
    edge = 0 if reverse else CHUNKS - 1
    for seq_no, (a, x) in enumerate(pieces):
        rows = rows_of(seq_no, CHUNKS)
        a_all = jnp.concatenate(a, axis=1)
        x_all = jnp.concatenate(x, axis=1)
        pre_ref[0, rows, :] = a_all
        pre_ref[1, rows, :] = x_all
        end_ref[seq_no : seq_no + 1, :] = a_all[edge : edge + 1]
        end_ref[count + seq_no : count + seq_no + 1, :] = x_all[edge : edge + 1]


def chunk_carries(pre_ref, carry_ref, count, reverse):
    reals, imags = [], []
    for seq_no in range(count):
        rows = rows_of(seq_no, CHUNKS)
        a = split(pre_ref[0, rows, :])
        x = split(pre_ref[1, rows, :])
        carry = split(carry_ref[seq_no : seq_no + 1, :])
        place = lax.broadcasted_iota(jnp.int32, a[0].shape, 0)
        first = place == (CHUNKS - 1 if reverse else 0)
        turn = CHUNKS - 1 if reverse else 1
        a = tuple(pltpu.roll(part, turn, 0) for part in a)
        x = tuple(pltpu.roll(part, turn, 0) for part in x)
        moved = times(a, carry)
        reals.append(jnp.where(first, carry[0], x[0] + moved[0]))
        imags.append(jnp.where(first, carry[1], x[1] + moved[1]))
    return jnp.concatenate(reals, axis=0), jnp.concatenate(imags, axis=0)


def chunk_factor(vec_ref, kept):
    group = kept.shape[0]
    whole = split(vec_ref[5:6, :])
    keep = wide(kept, whole[0].shape[-1])
    return tuple(spread_row(part, group) * keep for part in whole)


def lam_rows(vec_ref, group, conj=False):
    lam = split(vec_ref[4:5, :])
    real, imag = spread_row(lam[0], group), spread_row(lam[1], group)
    return (real, -imag) if conj else (real, imag)


def column_sums(value):
    return jnp.sum(value.reshape(-1, 8, value.shape[-1]), axis=0)


def drive_of(normed_low, in_re_ref, in_im_ref, vec_ref):
    gamma = vec_ref[3:4, :]
    half = gamma.shape[-1] // 2
    real = dot(normed_low, in_re_ref[0]) * gamma[:, :half]
    imag = dot(normed_low, in_im_ref[0]) * gamma[:, half:]
    return real, imag


def first_kernel(
    dims, resets_ref, tok_ref, in_re_ref, in_im_ref, vec_ref,
    drive_ref, keep_ref, kept_ref, pre_ref, end_ref, state_ref,
):
    count, group, steps, length = dims
    at = pl.program_id(0)
    states = in_re_ref.shape[-1]

    @pl.when(at == 0)
    def _():
        state_ref[...] = jnp.zeros_like(state_ref)
        kept_ref[...] = jnp.ones_like(kept_ref)

    place = lax.broadcasted_iota(jnp.int32, (CHUNKS, LANES), 0) * length + at * steps
    for step in range(steps):
        for seq_no in range(count):
            keep = jnp.ones((CHUNKS, LANES), F32)
            for slot in range(resets_ref.shape[1]):
                keep = jnp.where(place + step == resets_ref[seq_no, slot], 0.0, keep)
            start = step * group + seq_no * CHUNKS
            keep_ref[start : start + CHUNKS, :] = keep
    normed, _ = normalize(to_steps(tok_ref[...].astype(F32)))
    normed = normed * vec_ref[0:1, :] + vec_ref[1:2, :]
    drive = drive_of(normed.astype(BF16), in_re_ref, in_im_ref, vec_ref)
    drive_ref[:, :states] = drive[0]
    drive_ref[:, states:] = drive[1]
    end_of_block(dims, drive_ref, keep_ref, kept_ref, vec_ref, state_ref, pre_ref, end_ref, True)


def end_of_block(dims, drive_ref, keep_ref, kept_ref, vec_ref, state_ref, pre_ref, end_ref, track):
    count, group, steps, _ = dims
    if track:
        kept = kept_ref[...]
        for step in range(steps):
            kept = kept * keep_ref[rows_of(step, group), :]
        kept_ref[...] = kept
    state = split(state_ref[...])
    state = scan_up(drive_ref, keep_ref, lam_rows(vec_ref, group), state, steps, group)
    state_ref[...] = jnp.concatenate(state, axis=1)

    @pl.when(pl.program_id(0) == pl.num_programs(0) - 1)
    def _():
        factor = chunk_factor(vec_ref, kept_ref[...])
        pieces = chunk_totals(factor, split(state_ref[...]), count, False)
        write_totals(pieces, pre_ref, end_ref, False)


def layer_out(h_ref, normed, out_re_ref, out_im_ref, vec_ref, glu_w_ref, vec_glu):
    states = out_re_ref.shape[1]
    width = out_re_ref.shape[2]
    h_low = h_ref[...].astype(BF16)
    mixed = (
        dot(h_low[:, :states], out_re_ref[0])
        - dot(h_low[:, states:], out_im_ref[0])
        + vec_ref[2:3, :] * normed
    )
    act = (0.5 * mixed * (1.0 + gelu_tanh(mixed))).astype(BF16)
    value = dot(act, glu_w_ref[0, :, :width]) + vec_ref[9:10, :]
    gate = dot(act, glu_w_ref[0, :, width:]) + vec_ref[10:11, :]
    return mixed, value, gate


def second_kernel(
    dims, tok_ref, drive_ref, keep_ref, kept_ref, pre_in_ref, carry_ref,
    vec_ref, out_re_ref, out_im_ref, glu_w_ref, vec2_ref, in_re_ref, in_im_ref,
    h_ref, edge_ref, mixed_ref, value_ref, gate_ref, stream_ref, drive2_ref, pre_ref, end_ref,
    state_ref, state2_ref,
):
    count, group, steps, _ = dims
    states = in_re_ref.shape[-1]

    @pl.when(pl.program_id(0) == 0)
    def _():
        state_ref[...] = jnp.concatenate(chunk_carries(pre_in_ref, carry_ref, count, False), axis=1)
        state2_ref[...] = jnp.zeros_like(state2_ref)

    edge_ref[0] = state_ref[...]
    state = scan_up(
        drive_ref, keep_ref, lam_rows(vec_ref, group), split(state_ref[...]), steps, group, h_ref
    )
    state_ref[...] = jnp.concatenate(state, axis=1)
    stream = to_steps(tok_ref[...].astype(F32))
    normed, _ = normalize(stream)
    normed = normed * vec_ref[0:1, :] + vec_ref[1:2, :]
    mixed, value, gate = layer_out(
        h_ref, normed, out_re_ref, out_im_ref, vec_ref, glu_w_ref, None
    )
    mixed_ref[...] = mixed.astype(BF16)
    value_ref[...] = value.astype(BF16)
    gate_ref[...] = gate.astype(BF16)
    stream = stream + value * sigmoid(gate)
    stream_ref[...] = stream
    normed, _ = normalize(stream)
    normed = normed * vec2_ref[0:1, :] + vec2_ref[1:2, :]
    drive = drive_of(normed.astype(BF16), in_re_ref, in_im_ref, vec2_ref)
    drive2_ref[:, :states] = drive[0]
    drive2_ref[:, states:] = drive[1]
    end_of_block(
        dims, drive2_ref, keep_ref, kept_ref, vec2_ref, state2_ref, pre_ref, end_ref, False
    )


def gate_back(
    upstream, value, gate, mixed, h_low, out_re_ref, out_im_ref, glu_w_ref, sums_ref, grads_ref
):
    states = out_re_ref.shape[1]
    width = out_re_ref.shape[2]
    sig = sigmoid(gate)
    value_grad = upstream * sig
    gate_grad = (value_grad * value * (1.0 - sig)).astype(BF16)
    value_grad = value_grad.astype(BF16)
    sums_ref[:, 4 * width : 5 * width] += column_sums(value_grad.astype(F32))
    sums_ref[:, 5 * width : 6 * width] += column_sums(gate_grad.astype(F32))
    act_grad = dot_right_t(value_grad, glu_w_ref[0, :, :width]) + dot_right_t(
        gate_grad, glu_w_ref[0, :, width:]
    )
    bend = gelu_tanh(mixed)
    act = (0.5 * mixed * (1.0 + bend)).astype(BF16)
    mixed_low = (act_grad * gelu_slope(mixed, bend)).astype(BF16)
    grads_ref[:width, :] += dot_left_t(act, value_grad)
    grads_ref[width : 2 * width, :] += dot_left_t(act, gate_grad)
    base = 2 * width
    grads_ref[base : base + states, :] += dot_left_t(h_low[:, :states], mixed_low)
    grads_ref[base + states : base + 2 * states, :] -= dot_left_t(h_low[:, states:], mixed_low)
    return mixed_low, dot_right_t(mixed_low, out_re_ref[0]), -dot_right_t(mixed_low, out_im_ref[0])


def scan_down(dh_ref, keep_ref, lam, state, steps, group, base=0):
    states = lam[0].shape[-1]
    for step in range(steps - 1, -1, -1):
        rows = rows_of(step, group)
        if not isinstance(base, int):
            rows = pl.ds(base + step * group, group)
        keep = wide(keep_ref[rows, :], states)
        g = (dh_ref[rows, :states] + state[0], dh_ref[rows, states:] + state[1])
        state = times(lam, (keep * g[0], keep * g[1]))
    return state


def third_kernel(
    dims, stream_ref, drive_ref, keep_ref, keep_all_ref, kept_ref, cot_ref, pre_in_ref, carry_ref,
    vec_ref, out_re_ref, out_im_ref, glu_w_ref,
    act_ref, h_ref, edge_ref, mixed_grad_ref, dh_ref, pre_ref, end_ref, grads_ref, sums_ref,
    state_ref, dh_all_ref,
):
    count, group, steps, length = dims
    at = pl.program_id(0)
    states = out_re_ref.shape[1]

    @pl.when(at == 0)
    def _():
        state_ref[...] = jnp.concatenate(chunk_carries(pre_in_ref, carry_ref, count, False), axis=1)
        grads_ref[...] = jnp.zeros_like(grads_ref)
        sums_ref[...] = jnp.zeros_like(sums_ref)

    edge_ref[0] = state_ref[...]
    state = scan_up(
        drive_ref, keep_ref, lam_rows(vec_ref, group), split(state_ref[...]), steps, group, h_ref
    )
    state_ref[...] = jnp.concatenate(state, axis=1)
    stream = stream_ref[...]
    normed, _ = normalize(stream)
    normed = normed * vec_ref[0:1, :] + vec_ref[1:2, :]
    mixed, value, gate = layer_out(
        h_ref, normed, out_re_ref, out_im_ref, vec_ref, glu_w_ref, None
    )
    act_ref[...] = from_steps(stream + value * sigmoid(gate), group)
    upstream = to_steps(cot_ref[...])
    mixed_low, dh_re, dh_im = gate_back(
        upstream, value, gate, mixed, h_ref[...].astype(BF16),
        out_re_ref, out_im_ref, glu_w_ref, sums_ref, grads_ref,
    )
    mixed_grad_ref[...] = mixed_low
    dh_ref[:, :states] = dh_re
    dh_ref[:, states:] = dh_im
    size = steps * group
    base = pl.multiple_of(at * size, size)
    dh_all_ref[pl.ds(base, size), :states] = dh_re
    dh_all_ref[pl.ds(base, size), states:] = dh_im

    @pl.when(at == pl.num_programs(0) - 1)
    def _():
        lam = lam_rows(vec_ref, group, True)
        zero = jnp.zeros((group, states), F32)
        unroll = 16

        def turn(k, state):
            start = pl.multiple_of((length // unroll - 1 - k) * (unroll * group), unroll * group)
            return scan_down(dh_all_ref, keep_all_ref, lam, state, unroll, group, start)

        state = lax.fori_loop(0, length // unroll, turn, (zero, zero))
        factor = chunk_factor(vec_ref, kept_ref[...])
        pieces = chunk_totals((factor[0], -factor[1]), state, count, True)
        write_totals(pieces, pre_ref, end_ref, True)


def adjoint_part(
    dims, dh_ref, keep_ref, h_ref, edge_ref, drive_ref, stream, mixed_low, vec_ref,
    in_re_ref, in_im_ref, state_ref, g_ref, sums_ref, lam_sums_ref, grads_ref, grads_at,
):
    _, group, steps, _ = dims
    states = in_re_ref.shape[-1]
    width = in_re_ref.shape[1]
    lam = lam_rows(vec_ref, group, True)
    state = split(state_ref[...])
    lam_re, lam_im = split(lam_sums_ref[:, : 2 * states])
    gam = lam_sums_ref[:, 2 * states :]
    for step in range(steps - 1, -1, -1):
        rows = rows_of(step, group)
        keep = wide(keep_ref[rows, :], states)
        g = (dh_ref[rows, :states] + state[0], dh_ref[rows, states:] + state[1])
        kg = (keep * g[0], keep * g[1])
        state = times(lam, kg)
        g_ref[rows, :states] = g[0]
        g_ref[rows, states:] = g[1]
        if step > 0:
            before = rows_of(step - 1, group)
            prev = (h_ref[before, :states], h_ref[before, states:])
        else:
            prev = (edge_ref[0, :, :states], edge_ref[0, :, states:])
        lam_re = lam_re + (kg[0] * prev[0] + kg[1] * prev[1])
        lam_im = lam_im + (kg[1] * prev[0] - kg[0] * prev[1])
        gam = gam + (g[0] * drive_ref[rows, :states] + g[1] * drive_ref[rows, states:])
    state_ref[...] = jnp.concatenate(state, axis=1)
    lam_sums_ref[...] = jnp.concatenate([lam_re, lam_im, gam], axis=1)

    xhat, scale = normalize(stream)
    normed = xhat * vec_ref[0:1, :] + vec_ref[1:2, :]
    normed_low = normed.astype(BF16)
    drive_low = (g_ref[...] * vec_ref[3:4, :]).astype(BF16)
    grads_ref[grads_at : grads_at + width, :] += dot_left_t(normed_low, drive_low)
    mixed_wide = mixed_low.astype(F32)
    normed_grad = (
        dot_right_t(drive_low[:, :states], in_re_ref[0])
        + dot_right_t(drive_low[:, states:], in_im_ref[0])
        + vec_ref[2:3, :] * mixed_wide
    )
    sums_ref[:, :width] += column_sums(normed_grad * xhat)
    sums_ref[:, width : 2 * width] += column_sums(normed_grad)
    sums_ref[:, 3 * width : 4 * width] += column_sums(mixed_wide * normed)
    inner = normed_grad * vec_ref[0:1, :]
    middle = jnp.mean(inner, axis=-1, keepdims=True)
    along = jnp.mean(inner * xhat, axis=-1, keepdims=True)
    return scale * (inner - middle - xhat * along)


def finish_sums(small_ref, base, sums_ref, lam_sums_ref, vec_ref, states, width):
    total = jnp.sum(sums_ref[...], axis=0, keepdims=True)
    lam_total = jnp.sum(lam_sums_ref[...], axis=0, keepdims=True)
    lam_re, lam_im = lam_total[:, :states], lam_total[:, states : 2 * states]
    gam = lam_total[:, 2 * states :]
    nu_grad = (
        vec_ref[6:7, :states] * lam_re
        + vec_ref[6:7, states:] * lam_im
        + vec_ref[7:8, :states] * gam
    )
    theta_grad = vec_ref[8:9, :states] * lam_re + vec_ref[8:9, states:] * lam_im
    small_ref[base : base + 1, :] = total[:, :width]
    small_ref[base + 1 : base + 2, :] = total[:, width : 2 * width]
    small_ref[base + 2 : base + 3, :] = jnp.concatenate([nu_grad, theta_grad], axis=1)
    small_ref[base + 3 : base + 4, :] = total[:, 3 * width : 4 * width]
    small_ref[base + 4 : base + 5, :] = total[:, 4 * width : 5 * width]
    small_ref[base + 5 : base + 6, :] = total[:, 5 * width : 6 * width]


def fourth_kernel(
    dims, dh2_ref, keep_ref, kept_ref, h2_ref, edge2_ref, drive2_ref, stream_ref, mixed2_ref,
    cot_ref, sums2_ref, pre_in_ref, carry_ref, vec2_ref, in_re_ref, in_im_ref,
    value_ref, gate_ref, mixed_ref, h_ref, vec_ref, out_re_ref, out_im_ref, glu_w_ref,
    up_ref, mixed_grad_ref, dh_ref, pre_ref, end_ref, grads_ref, sums_ref, small_ref,
    state2_ref, state_ref, g_ref, run2_ref, lam2_ref,
):
    count, group, steps, _ = dims
    states = in_re_ref.shape[-1]
    width = in_re_ref.shape[1]
    at = pl.program_id(0)

    @pl.when(at == 0)
    def _():
        carries = chunk_carries(pre_in_ref, carry_ref, count, True)
        state2_ref[...] = jnp.concatenate(carries, axis=1)
        state_ref[...] = jnp.zeros_like(state_ref)
        grads_ref[...] = jnp.zeros_like(grads_ref)
        sums_ref[...] = jnp.zeros_like(sums_ref)
        run2_ref[...] = sums2_ref[...]
        lam2_ref[...] = jnp.zeros_like(lam2_ref)

    stream_grad = adjoint_part(
        dims, dh2_ref, keep_ref, h2_ref, edge2_ref, drive2_ref, stream_ref[...], mixed2_ref[...],
        vec2_ref, in_re_ref, in_im_ref, state2_ref, g_ref, run2_ref, lam2_ref, grads_ref,
        2 * width + 2 * states,
    )
    upstream = to_steps(cot_ref[...]) + stream_grad
    up_ref[...] = upstream
    mixed_low, dh_re, dh_im = gate_back(
        upstream, value_ref[...].astype(F32), gate_ref[...].astype(F32),
        mixed_ref[...].astype(F32), h_ref[...].astype(BF16),
        out_re_ref, out_im_ref, glu_w_ref, sums_ref, grads_ref,
    )
    mixed_grad_ref[...] = mixed_low
    dh_ref[:, :states] = dh_re
    dh_ref[:, states:] = dh_im
    lam = lam_rows(vec_ref, group, True)
    state = scan_down(dh_ref, keep_ref, lam, split(state_ref[...]), steps, group)
    state_ref[...] = jnp.concatenate(state, axis=1)

    @pl.when(at == pl.num_programs(0) - 1)
    def _():
        factor = chunk_factor(vec_ref, kept_ref[...])
        pieces = chunk_totals((factor[0], -factor[1]), split(state_ref[...]), count, True)
        write_totals(pieces, pre_ref, end_ref, True)
        small_ref[...] = jnp.zeros_like(small_ref)
        finish_sums(small_ref, 0, run2_ref, lam2_ref, vec2_ref, states, width)


def fifth_kernel(
    dims, dh_ref, keep_ref, h_ref, edge_ref, drive_ref, tok_ref, mixed_ref, up_ref, sums_in_ref,
    small_in_ref, pre_in_ref, carry_ref, vec_ref, in_re_ref, in_im_ref,
    grad_ref, grads_ref, small_ref, state_ref, g_ref, sums_ref, lam_ref,
):
    count, group, steps, _ = dims
    states = in_re_ref.shape[-1]
    width = in_re_ref.shape[1]
    at = pl.program_id(0)

    @pl.when(at == 0)
    def _():
        carries = chunk_carries(pre_in_ref, carry_ref, count, True)
        state_ref[...] = jnp.concatenate(carries, axis=1)
        grads_ref[...] = jnp.zeros_like(grads_ref)
        sums_ref[...] = sums_in_ref[...]
        lam_ref[...] = jnp.zeros_like(lam_ref)

    stream_grad = adjoint_part(
        dims, dh_ref, keep_ref, h_ref, edge_ref, drive_ref, to_steps(tok_ref[...].astype(F32)),
        mixed_ref[...], vec_ref, in_re_ref, in_im_ref, state_ref, g_ref, sums_ref, lam_ref,
        grads_ref, 0,
    )
    grad_ref[...] = from_steps(up_ref[...] + stream_grad, group)

    @pl.when(at == pl.num_programs(0) - 1)
    def _():
        small_ref[...] = small_in_ref[...]
        finish_sums(small_ref, 8, sums_ref, lam_ref, vec_ref, states, width)


def decay_rows(gain, bias, skip, nu_log, theta_log, glu_b, length):
    speed = jnp.exp(nu_log)
    phase = jnp.exp(theta_log)
    radius = jnp.exp(-speed)
    lam_re, lam_im = radius * jnp.cos(phase), radius * jnp.sin(phase)
    square = -jnp.expm1(-2.0 * speed)
    gamma = jnp.sqrt(square)
    far = jnp.exp(-speed * length)
    far_re, far_im = far * jnp.cos(phase * length), far * jnp.sin(phase * length)

    def pair(left, right):
        return jnp.concatenate([left, right], axis=-1)

    width = gain.shape[-1]
    rows = [
        gain,
        bias,
        skip,
        pair(gamma, gamma),
        pair(lam_re, lam_im),
        pair(far_re, far_im),
        pair(-speed * lam_re, -speed * lam_im),
        pair(speed * jnp.exp(-2.0 * speed) / square, jnp.zeros_like(speed)),
        pair(-phase * lam_im, phase * lam_re),
        glu_b[:, :width],
        glu_b[:, width:],
    ]
    rows += [jnp.zeros_like(gain)] * (16 - len(rows))
    return jnp.stack(rows, axis=1)


def combine_rows(first, second):
    count = first.shape[0] // 2
    first_a, first_x = split(first[:count]), split(first[count:])
    second_a, second_x = split(second[:count]), split(second[count:])
    factor = times(first_a, second_a)
    moved = times(second_a, first_x)
    value = (moved[0] + second_x[0], moved[1] + second_x[1])
    return jnp.concatenate(
        [jnp.concatenate(factor, axis=1), jnp.concatenate(value, axis=1)], axis=0
    )


def entering(total, axis, reverse):
    size, index = lax.axis_size(axis), lax.axis_index(axis)
    count = total.shape[0] // 2
    before = None
    bit = 1
    while bit < size:
        other = lax.ppermute(total, axis, [(i, i ^ bit) for i in range(size)])
        later = (index & bit) == 0 if reverse else (index & bit) != 0
        if before is None:
            joined = other
            identity = jnp.zeros_like(other).at[:count, : other.shape[1] // 2].set(1.0)
            before = jnp.where(later, joined, identity)
        else:
            before = jnp.where(later, combine_rows(other, before), before)
        if 2 * bit < size:
            total = jnp.where(later, combine_rows(other, total), combine_rows(total, other))
        bit *= 2
    return before[count:]


def flip(value, axes, sizes, bit):
    total = sizes[0] * sizes[1]
    return lax.ppermute(value, axes, [(i, i ^ (1 << bit)) for i in range(total)])


def linear_index(axes, sizes):
    return lax.axis_index(axes[0]) * sizes[1] + lax.axis_index(axes[1])


def reduce_parts(parts, orders, axes, sizes):
    index = linear_index(axes, sizes)
    for stage in range(len(orders[0])):
        sent = []
        for part, order in zip(parts, orders):
            upper = ((index >> order[stage]) & 1) == 1
            half = part.shape[0] // 2
            low, high = part[:half], part[half:]
            sent.append(
                (jnp.where(upper, high, low), flip(jnp.where(upper, low, high), axes, sizes, order[stage]))
            )
        parts = [mine + other for mine, other in sent]
    return parts


def gather_parts(parts, orders, axes, sizes):
    index = linear_index(axes, sizes)
    for stage in range(len(orders[0]) - 1, -1, -1):
        got = []
        for part, order in zip(parts, orders):
            upper = ((index >> order[stage]) & 1) == 1
            other = flip(part, axes, sizes, order[stage])
            got.append(
                jnp.concatenate(
                    [jnp.where(upper, other, part), jnp.where(upper, part, other)], axis=0
                )
            )
        parts = got
    return parts


def all_sum(value, axes, sizes):
    bits = (sizes[0] * sizes[1]).bit_length() - 1
    first = reduce_parts([value], [[0]], axes, sizes)[0]
    half = first.shape[0] // 2
    rest = list(range(1, bits))
    swapped = [rest[1], rest[0]] + rest[2:]
    orders = [rest, swapped]
    parts = reduce_parts([first[:half], first[half:]], orders, axes, sizes)
    parts = gather_parts(parts, orders, axes, sizes)
    return gather_parts([jnp.concatenate(parts, axis=0)], [[0]], axes, sizes)[0]


def all_sum_small(value, axes, sizes):
    bits = (sizes[0] * sizes[1]).bit_length() - 1
    for bit in range(bits):
        value = value + flip(value, axes, sizes, bit)
    return value


def shards(
    sizes, tokens, cotangent, resets, ln_gain, ln_bias, in_re, in_im, nu_log, theta_log,
    out_re, out_im, skip, glu_w, glu_b,
):
    axes = ("seq", "row")
    micro, rows_here, span, width = tokens.shape
    states = nu_log.shape[-1]
    count = micro * rows_here
    group = count * CHUNKS
    length = span // CHUNKS
    steps = 32 if length % 32 == 0 else length
    blocks = length // steps
    size = steps * group
    total = length * group
    dims = (count, group, steps, length)

    tok = tokens.reshape(group, length, width)
    cot = cotangent.reshape(group, length, width)
    starts = resets.reshape(count, -1) - lax.axis_index("seq") * span
    vec = decay_rows(ln_gain, ln_bias, skip, nu_log, theta_log, glu_b, length)

    def shape(*dims_, dtype=F32):
        return jax.ShapeDtypeStruct(dims_, dtype)

    def streamed(lanes, back=False):
        if back:
            return pl.BlockSpec((size, lanes), lambda i: (blocks - 1 - i, 0))
        return pl.BlockSpec((size, lanes), lambda i: (i, 0))

    def natural(back=False):
        if back:
            return pl.BlockSpec((group, steps, width), lambda i: (0, blocks - 1 - i, 0))
        return pl.BlockSpec((group, steps, width), lambda i: (0, i, 0))

    def edges(back=False):
        if back:
            return pl.BlockSpec((1, group, 2 * states), lambda i: (blocks - 1 - i, 0, 0))
        return pl.BlockSpec((1, group, 2 * states), lambda i: (i, 0, 0))

    def fixed(*dims_):
        return pl.BlockSpec(
            dims_, lambda i: (0,) * len(dims_), pipeline_mode=pl.Buffered(buffer_count=1)
        )

    def held(*dims_):
        return pl.BlockSpec(dims_, lambda i: (0,) * len(dims_))

    def layer(no, *dims_):
        return pl.BlockSpec(
            (1,) + dims_, lambda i: (no,) + (0,) * len(dims_),
            pipeline_mode=pl.Buffered(buffer_count=1),
        )

    def vec_of(no):
        return pl.BlockSpec(
            (None, 16, width), lambda i: (no, 0, 0), pipeline_mode=pl.Buffered(buffer_count=1)
        )

    def in_specs_of(no):
        return [layer(no, width, states), layer(no, width, states)]

    def out_specs_of(no):
        return [layer(no, states, width), layer(no, states, width)]

    def glu_spec(no):
        return layer(no, width, 2 * width)

    def call(kernel, in_specs, out_specs, out_shape, scratch):
        return pl.pallas_call(
            functools.partial(kernel, dims),
            grid=(blocks,),
            in_specs=in_specs,
            out_specs=out_specs,
            out_shape=out_shape,
            scratch_shapes=scratch,
            compiler_params=pltpu.CompilerParams(vmem_limit_bytes=VMEM_LIMIT),
        )

    two = 2 * states
    pre_spec, pre_shape = held(2, group, two), shape(2, group, two)
    end_spec, end_shape = held(2 * count, two), shape(2 * count, two)
    pre_in, carry_in = fixed(2, group, two), fixed(count, two)
    state = pltpu.VMEM((group, two), F32)

    drive1, keep, kept, pre1, end1 = call(
        first_kernel,
        [pl.BlockSpec(memory_space=pltpu.SMEM), natural()] + in_specs_of(0) + [vec_of(0)],
        [streamed(two), streamed(LANES), held(group, LANES), pre_spec, end_spec],
        [shape(total, two), shape(total, LANES), shape(group, LANES), pre_shape, end_shape],
        [state],
    )(starts, tok, in_re, in_im, vec)
    carry1 = entering(end1, "seq", False)

    h1, edge1, mixed1, value1, gate1, stream1, drive2, pre2, end2 = call(
        second_kernel,
        [natural(), streamed(two), streamed(LANES), fixed(group, LANES), pre_in, carry_in, vec_of(0)]
        + out_specs_of(0) + [glu_spec(0), vec_of(1)] + in_specs_of(1),
        [streamed(two), edges(), streamed(width), streamed(width), streamed(width), streamed(width),
         streamed(two), pre_spec, end_spec],
        [shape(total, two), shape(blocks, group, two), shape(total, width, dtype=BF16),
         shape(total, width, dtype=BF16), shape(total, width, dtype=BF16), shape(total, width),
         shape(total, two), pre_shape, end_shape],
        [state, state],
    )(tok, drive1, keep, kept, pre1, carry1, vec, out_re, out_im, glu_w, vec, in_re, in_im)
    carry2 = entering(end2, "seq", False)

    sums_spec, sums_shape = held(8, 6 * width), shape(8, 6 * width)
    act, h2, edge2, mixed_grad2, dh2, back2, back_end2, grads_a, sums2 = call(
        third_kernel,
        [streamed(width), streamed(two), streamed(LANES), fixed(total, LANES), fixed(group, LANES),
         natural(), pre_in, carry_in, vec_of(1)] + out_specs_of(1) + [glu_spec(1)],
        [natural(), streamed(two), edges(), streamed(width), streamed(two), pre_spec, end_spec,
         held(2 * width + two, width), sums_spec],
        [shape(group, length, width), shape(total, two), shape(blocks, group, two),
         shape(total, width, dtype=BF16), shape(total, two), pre_shape, end_shape,
         shape(2 * width + two, width), sums_shape],
        [state, pltpu.VMEM((total, two), F32)],
    )(stream1, drive2, keep, keep, kept, cot, pre2, carry2, vec, out_re, out_im, glu_w)
    back_carry2 = entering(back_end2, "seq", True)
    summed_a = all_sum(grads_a, axes, sizes)

    rows_b = 2 * width + two + width
    lam_sums = pltpu.VMEM((group, 3 * states), F32)
    run_sums = pltpu.VMEM((8, 6 * width), F32)
    up1, mixed_grad1, dh1, back1, back_end1, grads_b, sums1, small2 = call(
        fourth_kernel,
        [streamed(two, True), streamed(LANES, True), fixed(group, LANES), streamed(two, True),
         edges(True), streamed(two, True), streamed(width, True), streamed(width, True),
         natural(True), fixed(8, 6 * width), pre_in, carry_in, vec_of(1)] + in_specs_of(1)
        + [streamed(width, True), streamed(width, True), streamed(width, True), streamed(two, True),
           vec_of(0)] + out_specs_of(0) + [glu_spec(0)],
        [streamed(width, True), streamed(width, True), streamed(two, True), pre_spec, end_spec,
         held(rows_b, width), sums_spec, held(16, width)],
        [shape(total, width), shape(total, width, dtype=BF16), shape(total, two), pre_shape,
         end_shape, shape(rows_b, width), sums_shape, shape(16, width)],
        [state, state, pltpu.VMEM((size, two), F32), run_sums, lam_sums],
    )(dh2, keep, kept, h2, edge2, drive2, stream1, mixed_grad2, cot, sums2, back2, back_carry2, vec,
      in_re, in_im, value1, gate1, mixed1, h1, vec, out_re, out_im, glu_w)
    back_carry1 = entering(back_end1, "seq", True)
    summed_b = all_sum(grads_b, axes, sizes)

    input_grad, grads_c, small = call(
        fifth_kernel,
        [streamed(two, True), streamed(LANES, True), streamed(two, True), edges(True),
         streamed(two, True), natural(True), streamed(width, True), streamed(width, True),
         fixed(8, 6 * width), fixed(16, width), pre_in, carry_in, vec_of(0)] + in_specs_of(0),
        [natural(True), held(width, two), held(16, width)],
        [shape(group, length, width), shape(width, two), shape(16, width)],
        [state, pltpu.VMEM((size, two), F32), run_sums, lam_sums],
    )(dh1, keep, h1, edge1, drive1, tok, mixed_grad1, up1, sums1, small2, back1, back_carry1, vec,
      in_re, in_im)
    summed_c = all_sum(grads_c, axes, sizes)
    small = all_sum_small(small, axes, sizes)

    def two_layers(first, second):
        return jnp.stack([first, second])

    outs_at = 2 * width
    ins_at = outs_at + two
    small = small.reshape(2, 8, width)[::-1]
    grad_in2 = summed_b[ins_at:]
    return (
        act.reshape(tokens.shape),
        input_grad.reshape(tokens.shape),
        small[:, 0],
        small[:, 1],
        two_layers(summed_c[:, :states], grad_in2[:, :states]),
        two_layers(summed_c[:, states:], grad_in2[:, states:]),
        small[:, 2, :states],
        small[:, 2, states:],
        two_layers(summed_b[outs_at : outs_at + states], summed_a[outs_at : outs_at + states]),
        two_layers(summed_b[outs_at + states : ins_at], summed_a[outs_at + states : ins_at]),
        small[:, 3],
        jnp.concatenate(
            [
                two_layers(summed_b[:width], summed_a[:width]),
                two_layers(summed_b[width:outs_at], summed_a[width:outs_at]),
            ],
            axis=-1,
        ),
        small[:, 4:6].reshape(2, 2 * width),
    )


def solution(mesh):
    sizes = (mesh.shape["seq"], mesh.shape["row"])
    split_rows = P(None, "row", "seq", None)
    in_specs = (split_rows, split_rows, P(None, "row", None)) + (P(),) * 11
    out_specs = (split_rows, split_rows) + (P(),) * 11
    return jax.shard_map(
        functools.partial(shards, sizes),
        mesh=mesh,
        in_specs=in_specs,
        out_specs=out_specs,
        check_vma=False,
    )
```

time: 3730 us -> 322 us (0.09); the launches traced: 3660 us -> 321 us
  local copies, waits for them, and re-layouts: 2090 us -> 13.8 us
  other arithmetic: 747 us -> 33.5 us
  blocking collectives: 600 us -> 0 us
  starting transfers between devices: 0.04 us -> 93 us
  Pallas kernels: 0 us -> 88.4 us
  matrix products: 80.8 us -> 0 us
    slice x1141 -> x9, local copies, waits for them, and re-layouts: 1190 us -> 7.37 us  [the longest x2 1.92 us: shards(): small[:, 2, states:]]
    pad x576 -> x0, local copies, waits for them, and re-layouts: 671 us -> none  [the longest x288 426 us: layer_backward(): lax.associative_scan(combine, (next_real, next_imag, adj_real, adj_imag),...]
    all_gather x32 -> x0, blocking collectives: 559 us -> none  [entering(): everything = jax.tree.map(lambda part: lax.all_gather(part, axis), shard)]
    add x528 -> x44, other arithmetic: 438 us -> 9.52 us  [the longest x8 3.12 us: combine_rows(): value = (moved[0] + second_x[0], moved[1] + second_x[1])]
    concatenate x276 -> x23, other arithmetic: 173 us -> 6.3 us  [the longest x3 3.62 us: all_sum(): return gather_parts([jnp.concatenate(parts, axis=0)], [[0]], axes, sizes)[0]]
    rev x16 -> x0, local copies, waits for them, and re-layouts: 123 us -> none  [layer_backward(): lax.associative_scan(combine, (next_real, next_imag, adj_real, adj_imag),...]
    psum x1 -> x0, waiting for transfers between devices: 110 us -> none  [shards(): lax.psum((grad_gain, grad_bias, grad_in_real, grad_in_imag, grad_nu, grad...]
    ppermute x0 -> x71, starting transfers between devices: none -> 93 us  [the longest x59 64.1 us: flip(): return lax.ppermute(value, axes, [(i, i ^ 1 << bit) for i in range(total)])]
where the time goes in v1:
time: 322 us; the launch traced here: 321 us
  starting transfers between devices  93 us (29%)
  waiting for transfers between devices  90.7 us (28%)
  Pallas kernels  88.4 us (27%)
  other arithmetic  33.5 us (10%)
  local copies, waits for them, and re-layouts  13.8 us (4%)
    ppermute x59, waiting for transfers between devices, flip(): return lax.ppermute(value, axes, [(i, i ^ 1 << bit) for i in range(total)])  69.6 us
    ppermute x59, starting transfers between devices, flip(): return lax.ppermute(value, axes, [(i, i ^ 1 << bit) for i in range(total)])  64.1 us
    ppermute x12, starting transfers between devices, entering(): other = lax.ppermute(total, axis, [(i, i ^ bit) for i in range(size)])  28.9 us
    pallas_call x1, Pallas kernels, shards(): call(fourth_kernel, [streamed(two, True), streamed(LANES, True), fixed(gr...  27.9 us
    pallas_call x1, Pallas kernels, shards(): call(third_kernel, [streamed(width), streamed(two), streamed(LANES), fixe...  23.7 us
    ppermute x12, waiting for transfers between devices, entering(): other = lax.ppermute(total, axis, [(i, i ^ bit) for i in range(size)])  21.1 us
    pallas_call x1, Pallas kernels, shards(): call(second_kernel, [natural(), streamed(two), streamed(LANES), fixed(gro...  15.1 us
    pallas_call x1, Pallas kernels, shards(): call(fifth_kernel, [streamed(two, True), streamed(LANES, True), streamed(...  14.6 us
  transfers between devices with their start and end apart: 71, of which 54 were waited for; matrix products, arithmetic and copies ran while one was open for 7% of the time, Pallas kernels for 0%

profile of v1, /device:TPU:0, one launch (start us, length us, event | category | flops | bytes accessed | tf_op | source)
XLA Modules:
  0.0 321.2 jit_solution(3092262869887710633)
XLA Ops:
  6.9 7.1 %shard_map.237 = (f32[2048,512]{1,0:T(8,128)}, f32[2048,128]{1,0:T(8,128)}, f32[16,128]{1,0:T(8,128)}, f32[2,16,512]{2,1,0:T(8,128)}, f32[4,512]{1,0:T(4,128)}) custom-call(s32[2,8]{1,0:T(2,128)} %bitcast.59, bf16[16,128,512]{2,1,0:T(8,128)(2,1)} %bitcast.53, bf16[2,512,256]{2,1,0:T(8,128)(2,1)} %in_re_ref.7, bf16[2,512,256]{2,1,0:T(8,128)(2,1)} %in_im_ref.7, ...), custom_call_target="tpu_custom_call" | custom-call | tf_op jit(solution)/shard_map/pallas_call | solution.py:731
  14.1 3.0 collective-permute-start
  17.1 1.8 collective-permute-done
  20.5 2.1 collective-permute-start.1
  24.3 3.1 collective-permute-start.2
  29.7 15.1 %shard_map.238 = (f32[2048,512]{1,0:T(8,128)}, f32[4,16,512]{2,1,0:T(8,128)}, bf16[2048,512]{1,0:T(8,128)(2,1)}, bf16[2048,512]{1,0:T(8,128)(2,1)}, bf16[2048,51...) custom-call(bf16[16,128,512]{2,1,0:T(8,128)(2,1)} %bitcast.54, ...), custom_call_target="tpu_custom_call" | custom-call | tf_op jit(solution)/shard_map/pallas_call | solution.py:740
  44.8 1.9 collective-permute-start.3
  46.7 2.0 collective-permute-done.3
  50.3 2.0 collective-permute-start.4
  54.1 3.0 collective-permute-start.5
  59.3 23.7 %shard_map.239 = (f32[16,128,512]{2,1,0:T(8,128)}, f32[2048,512]{1,0:T(8,128)}, f32[4,16,512]{2,1,0:T(8,128)}, bf16[2048,512]{1,0:T(8,128)(2,1)}, f32[2048,512]{...) custom-call(f32[2048,512]{1,0:T(8,128)} %get-tuple-element.88.stream_ref, ...), custom_call_target="tpu_custom_call" | custom-call | tf_op jit(solution)/shard_map/pallas_call | solution.py:754
  83.0 1.9 collective-permute-start.6
  84.9 2.0 collective-permute-done.6
  88.5 2.0 collective-permute-start.7
  92.3 3.0 collective-permute-start.8
  97.5 27.9 %shard_map.240 = (f32[2048,512]{1,0:T(8,128)}, bf16[2048,512]{1,0:T(8,128)(2,1)}, f32[2048,512]{1,0:T(8,128)}, f32[2,16,512]{2,1,0:T(8,128)}, f32[4,512]{1,0:T(4...) custom-call(f32[2048,512]{1,0:T(8,128)} %get-tuple-element.93.dh2_ref, ...), custom_call_target="tpu_custom_call" | custom-call | tf_op jit(solution)/shard_map/pallas_call | solution.py:771
  125.4 1.9 collective-permute-start.9
  127.3 2.0 collective-permute-done.9
  130.9 2.0 collective-permute-start.10
  134.6 3.0 collective-permute-start.11
  139.9 14.6 %shard_map.241 = (f32[16,128,512]{2,1,0:T(8,128)}, f32[512,512]{1,0:T(8,128)}, f32[16,512]{1,0:T(8,128)}) custom-call(f32[2048,512]{1,0:T(8,128)} %get-tuple-element.104.dh_ref, f32[2048,128]{1,0:T(8,128)} %get-tuple-element.84.keep_ref.keep_all_ref, f32[2048,512]{1,0:T(8,128)} %get-tuple-element.103.h_ref, f32[4,16,512]{2,1,0:T(8,128)} %get-tuple-element.105.edge_ref, ...), custom_call_target="tpu_custom_call" | custom-call | tf_op jit(solution)/shard_map/pallas_call | solution.py:788
  156.7 1.8 collective-permute-start.13
  160.6 1.8 collective-permute-start.14
  164.6 1.9 collective-permute-start.15
  168.5 2.9 collective-permute-start.16
  174.7 1.9 collective-permute-done.18
  180.4 2.1 collective-permute-done.27
  182.5 2.4 collective-permute-start.28
  185.0 1.8 collective-permute-done.28
  187.2 1.8 collective-permute-done.20
  196.1 2.1 collective-permute-start.31
  200.5 1.9 collective-permute-done.23
  208.5 1.8 collective-permute-start.25
  211.7 7.7 %collective-permute-done.54 = f32[192,512]{1,0:T(8,128)S(1)} collective-permute-done((f32[192,512]{1,0:T(8,128)S(1)}, f32[192,512]{1,0:T(8,128)S(1)}, u32[]{:S(2)}, u32[]{:S(2)}) %collective-permute-start.54) | collective-permute-done | bytes 393248 | tf_op jit(solution)/shard_map/ppermute | solution.py:590
  234.0 2.0 collective-permute-done.65
  239.2 2.0 collective-permute-done.66
  241.1 1.8 collective-permute-start.67
  259.8 2.8 collective-permute-done.46
  265.8 2.3 collective-permute-done.47
  271.2 2.2 collective-permute-done.48
  273.5 2.0 collective-permute-done.40
  275.6 2.8 collective-permute-done.49
  281.5 3.5 %collective-permute-done.50 = f32[128,512]{1,0:T(8,128)S(1)} collective-permute-done((f32[128,512]{1,0:T(8,128)S(1)}, f32[128,512]{1,0:T(8,128)S(1)}, u32[]{:S(2)}, u32[]{:S(2)}) %collective-permute-start.50) | collective-permute-done | bytes 262176 | tf_op jit(solution)/shard_map/ppermute | solution.py:590
  289.8 4.5 %collective-permute-done.51 = f32[256,512]{1,0:T(8,128)S(1)} collective-permute-done((f32[256,512]{1,0:T(8,128)S(1)}, f32[256,512]{1,0:T(8,128)S(1)}, u32[]{:S(2)}, u32[]{:S(2)}) %collective-permute-start.51) | collective-permute-done | bytes 524320 | tf_op jit(solution)/shard_map/ppermute | solution.py:590
  294.4 2.0 collective-permute-done.43
  310.1 1.8 broadcast_select_fusion.2
  312.1 2.1 broadcast_select_fusion
  318.8 2.4 maximum_maximum_fusion
  (308 shorter events, 128.3 us)
Async XLA Ops:
  14.1 4.9 %collective-permute-start = (f32[4,512]{1,0:T(4,128)}, f32[4,512]{1,0:T(4,128)S(1)}, u32[]{:S(2)}, u32[]{:S(2)}) collective-permute-start(f32[4,512]{1,0:T(4,128)} %get-tuple-element.87), channel_id=1, source_target_pairs={{0,4},{4,0},{8,12},{12,8},{16,20},{20,16},{24,28},{28,24},{1,5},{5... | collective-permute-start | bytes 24584 | tf_op jit(solution)/shard_map/ppermute | solution.py:574
  24.3 4.7 %collective-permute-start.2 = (f32[4,512]{1,0:T(4,128)S(1)}, f32[4,512]{1,0:T(4,128)S(1)}, u32[]{:S(2)}, u32[]{:S(2)}) collective-permute-start(f32[4,512]{1,0:T(4,128)S(1)} %maximum_select_fusion.1), channel_id=1, source_target_pairs={{0,16},{4,20},{8,24},{12,28},{16,0},{20,4},{24,8},{28,12},{1,17},{... | collective-permute-start | bytes 24584 | tf_op jit(solution)/shard_map/ppermute | solution.py:574
  159.8 11.6 %collective-permute-start.17 = (f32[256,512]{1,0:T(8,128)S(1)}, f32[256,512]{1,0:T(8,128)S(1)}, u32[]{:S(2)}, u32[]{:S(2)}) collective-permute-start(f32[256,512]{1,0:T(8,128)S(1)} %slice_select_fusion.4), channel_id=1, source_target_pairs={{0,1},{1,0},{2,3},{3,2},{4,5},{5,4},{6,7},{7,6},{8,9},{9,8},{10,11... | collective-permute-start | bytes 1572872 | tf_op jit(solution)/shard_map/ppermute | solution.py:590
  162.8 43.8 %collective-permute-start.53 = (f32[768,512]{1,0:T(8,128)S(1)}, f32[768,512]{1,0:T(8,128)S(1)}, u32[]{:S(2)}, u32[]{:S(2)}) collective-permute-start(f32[768,512]{1,0:T(8,128)S(1)} %slice_select_fusion.1), channel_id=1, source_target_pairs={{0,1},{1,0},{2,3},{3,2},{4,5},{5,4},{6,7},{7,6},{8,9},{9,8},{10,11... | collective-permute-start | bytes 4718600 | tf_op jit(solution)/shard_map/ppermute | solution.py:590
  166.9 55.7 %collective-permute-start.35 = (f32[1024,512]{1,0:T(8,128)S(1)}, f32[1024,512]{1,0:T(8,128)S(1)}, u32[]{:S(2)}, u32[]{:S(2)}) collective-permute-start(f32[1024,512]{1,0:T(8,128)S(1)} %slice_select_fusion), channel_id=1, source_target_pairs={{0,1},{1,0},{2,3},{3,2},{4,5},{5,4},{6,7},{7,6},{8,9},{9,8},{10,11... | collective-permute-start | bytes 6291464 | tf_op jit(solution)/shard_map/ppermute | solution.py:590
  168.5 6.2 %collective-permute-start.16 = (f32[16,512]{1,0:T(8,128)S(1)}, f32[16,512]{1,0:T(8,128)S(1)}, u32[]{:S(2)}, u32[]{:S(2)}) collective-permute-start(f32[16,512]{1,0:T(8,128)S(1)} %add.482), channel_id=1, source_target_pairs={{0,16},{1,17},{2,18},{3,19},{4,20},{5,21},{6,22},{7,23},{8,24},{9,... | collective-permute-start | bytes 98312 | tf_op jit(solution)/shard_map/ppermute | solution.py:590
  171.6 5.0 %collective-permute-start.18 = (f32[64,512]{1,0:T(8,128)S(1)}, f32[64,512]{1,0:T(8,128)S(1)}, u32[]{:S(2)}, u32[]{:S(2)}) collective-permute-start(f32[64,512]{1,0:T(8,128)S(1)} %get-tuple-element.166), channel_id=1, source_target_pairs={{0,2},{1,3},{2,0},{3,1},{4,6},{5,7},{6,4},{7,5},{8,10},{9,11},{10,... | collective-permute-start | bytes 393224 | tf_op jit(solution)/shard_map/ppermute | solution.py:590
  173.1 5.0 %collective-permute-start.26 = (f32[64,512]{1,0:T(8,128)S(1)}, f32[64,512]{1,0:T(8,128)S(1)}, u32[]{:S(2)}, u32[]{:S(2)}) collective-permute-start(f32[64,512]{1,0:T(8,128)S(1)} %get-tuple-element.167), channel_id=1, source_target_pairs={{0,4},{1,5},{2,6},{3,7},{4,0},{5,1},{6,2},{7,3},{8,12},{9,13},{10,... | collective-permute-start | bytes 393224 | tf_op jit(solution)/shard_map/ppermute | solution.py:590
  178.8 6.1 %collective-permute-start.19 = (f32[32,512]{1,0:T(8,128)S(1)}, f32[32,512]{1,0:T(8,128)S(1)}, u32[]{:S(2)}, u32[]{:S(2)}) collective-permute-start(f32[32,512]{1,0:T(8,128)S(1)} %slice_select_fusion.20), channel_id=1, source_target_pairs={{0,4},{1,5},{2,6},{3,7},{4,0},{5,1},{6,2},{7,3},{8,12},{9,13},{10,... | collective-permute-start | bytes 196616 | tf_op jit(solution)/shard_map/ppermute | solution.py:590
  186.8 4.7 %collective-permute-start.29 = (f32[8,512]{1,0:T(8,128)S(1)}, f32[8,512]{1,0:T(8,128)S(1)}, u32[]{:S(2)}, u32[]{:S(2)}) collective-permute-start(f32[8,512]{1,0:T(8,128)S(1)} %slice_select_fusion.25), channel_id=1, source_target_pairs={{0,16},{1,17},{2,18},{3,19},{4,20},{5,21},{6,22},{7,23},{8,24},{9,... | collective-permute-start | bytes 49160 | tf_op jit(solution)/shard_map/ppermute | solution.py:590
  189.1 4.7 %collective-permute-start.21 = (f32[8,512]{1,0:T(8,128)S(1)}, f32[8,512]{1,0:T(8,128)S(1)}, u32[]{:S(2)}, u32[]{:S(2)}) collective-permute-start(f32[8,512]{1,0:T(8,128)S(1)} %slice_select_fusion.26), channel_id=1, source_target_pairs={{0,16},{1,17},{2,18},{3,19},{4,20},{5,21},{6,22},{7,23},{8,24},{9,... | collective-permute-start | bytes 49160 | tf_op jit(solution)/shard_map/ppermute | solution.py:590
  200.2 5.1 %collective-permute-start.32 = (f32[32,512]{1,0:T(8,128)S(1)}, f32[32,512]{1,0:T(8,128)S(1)}, u32[]{:S(2)}, u32[]{:S(2)}) collective-permute-start(f32[32,512]{1,0:T(8,128)S(1)} %pad_maximum_fusion.24), channel_id=1, source_target_pairs={{0,2},{1,3},{2,0},{3,1},{4,6},{5,7},{6,4},{7,5},{8,10},{9,11},{10,... | collective-permute-start | bytes 196616 | tf_op jit(solution)/shard_map/ppermute | solution.py:590
  202.5 6.0 %collective-permute-start.24 = (f32[32,512]{1,0:T(8,128)S(1)}, f32[32,512]{1,0:T(8,128)S(1)}, u32[]{:S(2)}, u32[]{:S(2)}) collective-permute-start(f32[32,512]{1,0:T(8,128)S(1)} %pad_maximum_fusion.23), channel_id=1, source_target_pairs={{0,4},{1,5},{2,6},{3,7},{4,0},{5,1},{6,2},{7,3},{8,12},{9,13},{10,... | collective-permute-start | bytes 196616 | tf_op jit(solution)/shard_map/ppermute | solution.py:590
  205.3 6.4 %collective-permute-start.33 = (f32[64,512]{1,0:T(8,128)S(1)}, f32[64,512]{1,0:T(8,128)S(1)}, u32[]{:S(2)}, u32[]{:S(2)}) collective-permute-start(f32[64,512]{1,0:T(8,128)S(1)} %pad_maximum_fusion.18), channel_id=1, source_target_pairs={{0,4},{1,5},{2,6},{3,7},{4,0},{5,1},{6,2},{7,3},{8,12},{9,13},{10,... | collective-permute-start | bytes 393224 | tf_op jit(solution)/shard_map/ppermute | solution.py:590
  207.2 12.1 %collective-permute-start.54 = (f32[192,512]{1,0:T(8,128)S(1)}, f32[192,512]{1,0:T(8,128)S(1)}, u32[]{:S(2)}, u32[]{:S(2)}) collective-permute-start(f32[192,512]{1,0:T(8,128)S(1)} %get-tuple-element.150), channel_id=1, source_target_pairs={{0,2},{1,3},{2,0},{3,1},{4,6},{5,7},{6,4},{7,5},{8,10},{9,11},{10,... | collective-permute-start | bytes 1179656 | tf_op jit(solution)/shard_map/ppermute | solution.py:590
  207.6 12.5 %collective-permute-start.62 = (f32[192,512]{1,0:T(8,128)S(1)}, f32[192,512]{1,0:T(8,128)S(1)}, u32[]{:S(2)}, u32[]{:S(2)}) collective-permute-start(f32[192,512]{1,0:T(8,128)S(1)} %get-tuple-element.151), channel_id=1, source_target_pairs={{0,4},{1,5},{2,6},{3,7},{4,0},{5,1},{6,2},{7,3},{8,12},{9,13},{10,... | collective-permute-start | bytes 1179656 | tf_op jit(solution)/shard_map/ppermute | solution.py:590
  208.5 89.5 %collective-permute-start.25 = (f32[64,512]{1,0:T(8,128)S(1)}, f32[64,512]{1,0:T(8,128)S(1)}, u32[]{:S(2)}, u32[]{:S(2)}) collective-permute-start(f32[64,512]{1,0:T(8,128)S(1)} %pad_maximum_fusion.17), channel_id=1, source_target_pairs={{0,2},{1,3},{2,0},{3,1},{4,6},{5,7},{6,4},{7,5},{8,10},{9,11},{10,... | collective-permute-start | bytes 393224 | tf_op jit(solution)/shard_map/ppermute | solution.py:590
  220.4 5.7 %collective-permute-start.63 = (f32[96,512]{1,0:T(8,128)S(1)}, f32[96,512]{1,0:T(8,128)S(1)}, u32[]{:S(2)}, u32[]{:S(2)}) collective-permute-start(f32[96,512]{1,0:T(8,128)S(1)} %slice_select_fusion.9), channel_id=1, source_target_pairs={{0,2},{1,3},{2,0},{3,1},{4,6},{5,7},{6,4},{7,5},{8,10},{9,11},{10,... | collective-permute-start | bytes 589832 | tf_op jit(solution)/shard_map/ppermute | solution.py:590
  221.8 5.8 %collective-permute-start.55 = (f32[96,512]{1,0:T(8,128)S(1)}, f32[96,512]{1,0:T(8,128)S(1)}, u32[]{:S(2)}, u32[]{:S(2)}) collective-permute-start(f32[96,512]{1,0:T(8,128)S(1)} %slice_select_fusion.10), channel_id=1, source_target_pairs={{0,4},{1,5},{2,6},{3,7},{4,0},{5,1},{6,2},{7,3},{8,12},{9,13},{10,... | collective-permute-start | bytes 589832 | tf_op jit(solution)/shard_map/ppermute | solution.py:590
  223.6 27.1 %collective-permute-start.36 = (f32[256,512]{1,0:T(8,128)S(1)}, f32[256,512]{1,0:T(8,128)S(1)}, u32[]{:S(2)}, u32[]{:S(2)}) collective-permute-start(f32[256,512]{1,0:T(8,128)S(1)} %get-tuple-element.142), channel_id=1, source_target_pairs={{0,2},{1,3},{2,0},{3,1},{4,6},{5,7},{6,4},{7,5},{8,10},{9,11},{10,... | collective-permute-start | bytes 1572872 | tf_op jit(solution)/shard_map/ppermute | solution.py:590
  224.9 25.8 %collective-permute-start.44 = (f32[256,512]{1,0:T(8,128)S(1)}, f32[256,512]{1,0:T(8,128)S(1)}, u32[]{:S(2)}, u32[]{:S(2)}) collective-permute-start(f32[256,512]{1,0:T(8,128)S(1)} %get-tuple-element.143), channel_id=1, source_target_pairs={{0,4},{1,5},{2,6},{3,7},{4,0},{5,1},{6,2},{7,3},{8,12},{9,13},{10,... | collective-permute-start | bytes 1572872 | tf_op jit(solution)/shard_map/ppermute | solution.py:590
  226.2 4.7 %collective-permute-start.64 = (f32[48,512]{1,0:T(8,128)S(1)}, f32[48,512]{1,0:T(8,128)S(1)}, u32[]{:S(2)}, u32[]{:S(2)}) collective-permute-start(f32[48,512]{1,0:T(8,128)S(1)} %slice_select_fusion.15), channel_id=1, source_target_pairs={{0,8},{1,9},{2,10},{3,11},{4,12},{5,13},{6,14},{7,15},{8,0},{9,1},... | collective-permute-start | bytes 294920 | tf_op jit(solution)/shard_map/ppermute | solution.py:590
  230.9 5.1 %collective-permute-start.65 = (f32[24,512]{1,0:T(8,128)S(1)}, f32[24,512]{1,0:T(8,128)S(1)}, u32[]{:S(2)}, u32[]{:S(2)}) collective-permute-start(f32[24,512]{1,0:T(8,128)S(1)} %slice_select_fusion.21), channel_id=1, source_target_pairs={{0,16},{1,17},{2,18},{3,19},{4,20},{5,21},{6,22},{7,23},{8,24},{9,... | collective-permute-start | bytes 147464 | tf_op jit(solution)/shard_map/ppermute | solution.py:590
  232.4 5.1 %collective-permute-start.57 = (f32[24,512]{1,0:T(8,128)S(1)}, f32[24,512]{1,0:T(8,128)S(1)}, u32[]{:S(2)}, u32[]{:S(2)}) collective-permute-start(f32[24,512]{1,0:T(8,128)S(1)} %slice_select_fusion.22), channel_id=1, source_target_pairs={{0,16},{1,17},{2,18},{3,19},{4,20},{5,21},{6,22},{7,23},{8,24},{9,... | collective-permute-start | bytes 147464 | tf_op jit(solution)/shard_map/ppermute | solution.py:590
  236.0 5.2 %collective-permute-start.66 = (f32[24,512]{1,0:T(8,128)S(1)}, f32[24,512]{1,0:T(8,128)S(1)}, u32[]{:S(2)}, u32[]{:S(2)}) collective-permute-start(f32[24,512]{1,0:T(8,128)S(1)} %select_add_fusion.21), channel_id=1, source_target_pairs={{0,16},{1,17},{2,18},{3,19},{4,20},{5,21},{6,22},{7,23},{8,24},{9,... | collective-permute-start | bytes 147464 | tf_op jit(solution)/shard_map/ppermute | solution.py:590
  237.5 5.5 %collective-permute-start.58 = (f32[24,512]{1,0:T(8,128)S(1)}, f32[24,512]{1,0:T(8,128)S(1)}, u32[]{:S(2)}, u32[]{:S(2)}) collective-permute-start(f32[24,512]{1,0:T(8,128)S(1)} %select_add_fusion.22), channel_id=1, source_target_pairs={{0,16},{1,17},{2,18},{3,19},{4,20},{5,21},{6,22},{7,23},{8,24},{9,... | collective-permute-start | bytes 147464 | tf_op jit(solution)/shard_map/ppermute | solution.py:590
  243.0 5.9 %collective-permute-start.59 = (f32[48,512]{1,0:T(8,128)S(1)}, f32[48,512]{1,0:T(8,128)S(1)}, u32[]{:S(2)}, u32[]{:S(2)}) collective-permute-start(f32[48,512]{1,0:T(8,128)S(1)} %pad_maximum_fusion.21), channel_id=1, source_target_pairs={{0,8},{1,9},{2,10},{3,11},{4,12},{5,13},{6,14},{7,15},{8,0},{9,1},... | collective-permute-start | bytes 294920 | tf_op jit(solution)/shard_map/ppermute | solution.py:590
  245.9 7.4 %collective-permute-start.68 = (f32[96,512]{1,0:T(8,128)S(1)}, f32[96,512]{1,0:T(8,128)S(1)}, u32[]{:S(2)}, u32[]{:S(2)}) collective-permute-start(f32[96,512]{1,0:T(8,128)S(1)} %pad_maximum_fusion.16), channel_id=1, source_target_pairs={{0,2},{1,3},{2,0},{3,1},{4,6},{5,7},{6,4},{7,5},{8,10},{9,11},{10,... | collective-permute-start | bytes 589832 | tf_op jit(solution)/shard_map/ppermute | solution.py:590
  249.0 5.7 %collective-permute-start.60 = (f32[96,512]{1,0:T(8,128)S(1)}, f32[96,512]{1,0:T(8,128)S(1)}, u32[]{:S(2)}, u32[]{:S(2)}) collective-permute-start(f32[96,512]{1,0:T(8,128)S(1)} %pad_maximum_fusion.15), channel_id=1, source_target_pairs={{0,4},{1,5},{2,6},{3,7},{4,0},{5,1},{6,2},{7,3},{8,12},{9,13},{10,... | collective-permute-start | bytes 589832 | tf_op jit(solution)/shard_map/ppermute | solution.py:590
  251.0 6.4 %collective-permute-start.45 = (f32[128,512]{1,0:T(8,128)S(1)}, f32[128,512]{1,0:T(8,128)S(1)}, u32[]{:S(2)}, u32[]{:S(2)}) collective-permute-start(f32[128,512]{1,0:T(8,128)S(1)} %slice_select_fusion.7), channel_id=1, source_target_pairs={{0,2},{1,3},{2,0},{3,1},{4,6},{5,7},{6,4},{7,5},{8,10},{9,11},{10,... | collective-permute-start | bytes 786440 | tf_op jit(solution)/shard_map/ppermute | solution.py:590
  251.5 6.4 %collective-permute-start.37 = (f32[128,512]{1,0:T(8,128)S(1)}, f32[128,512]{1,0:T(8,128)S(1)}, u32[]{:S(2)}, u32[]{:S(2)}) collective-permute-start(f32[128,512]{1,0:T(8,128)S(1)} %slice_select_fusion.8), channel_id=1, source_target_pairs={{0,4},{1,5},{2,6},{3,7},{4,0},{5,1},{6,2},{7,3},{8,12},{9,13},{10,... | collective-permute-start | bytes 786440 | tf_op jit(solution)/shard_map/ppermute | solution.py:590
  253.3 12.5 %collective-permute-start.69 = (f32[192,512]{1,0:T(8,128)S(1)}, f32[192,512]{1,0:T(8,128)S(1)}, u32[]{:S(2)}, u32[]{:S(2)}) collective-permute-start(f32[192,512]{1,0:T(8,128)S(1)} %pad_maximum_fusion.12), channel_id=1, source_target_pairs={{0,4},{1,5},{2,6},{3,7},{4,0},{5,1},{6,2},{7,3},{8,12},{9,13},{10,... | collective-permute-start | bytes 1179656 | tf_op jit(solution)/shard_map/ppermute | solution.py:590
  254.8 33.6 %collective-permute-start.61 = (f32[192,512]{1,0:T(8,128)S(1)}, f32[192,512]{1,0:T(8,128)S(1)}, u32[]{:S(2)}, u32[]{:S(2)}) collective-permute-start(f32[192,512]{1,0:T(8,128)S(1)} %pad_maximum_fusion.11), channel_id=1, source_target_pairs={{0,2},{1,3},{2,0},{3,1},{4,6},{5,7},{6,4},{7,5},{8,10},{9,11},{10,... | collective-permute-start | bytes 1179656 | tf_op jit(solution)/shard_map/ppermute | solution.py:590
  257.6 5.0 %collective-permute-start.46 = (f32[64,512]{1,0:T(8,128)S(1)}, f32[64,512]{1,0:T(8,128)S(1)}, u32[]{:S(2)}, u32[]{:S(2)}) collective-permute-start(f32[64,512]{1,0:T(8,128)S(1)} %slice_select_fusion.11), channel_id=1, source_target_pairs={{0,8},{1,9},{2,10},{3,11},{4,12},{5,13},{6,14},{7,15},{8,0},{9,1},... | collective-permute-start | bytes 393224 | tf_op jit(solution)/shard_map/ppermute | solution.py:590
  258.0 5.9 %collective-permute-start.38 = (f32[64,512]{1,0:T(8,128)S(1)}, f32[64,512]{1,0:T(8,128)S(1)}, u32[]{:S(2)}, u32[]{:S(2)}) collective-permute-start(f32[64,512]{1,0:T(8,128)S(1)} %slice_select_fusion.12), channel_id=1, source_target_pairs={{0,8},{1,9},{2,10},{3,11},{4,12},{5,13},{6,14},{7,15},{8,0},{9,1},... | collective-permute-start | bytes 393224 | tf_op jit(solution)/shard_map/ppermute | solution.py:590
  262.6 5.5 %collective-permute-start.47 = (f32[32,512]{1,0:T(8,128)S(1)}, f32[32,512]{1,0:T(8,128)S(1)}, u32[]{:S(2)}, u32[]{:S(2)}) collective-permute-start(f32[32,512]{1,0:T(8,128)S(1)} %slice_select_fusion.17), channel_id=1, source_target_pairs={{0,16},{1,17},{2,18},{3,19},{4,20},{5,21},{6,22},{7,23},{8,24},{9,... | collective-permute-start | bytes 196616 | tf_op jit(solution)/shard_map/ppermute | solution.py:590
  264.0 5.9 %collective-permute-start.39 = (f32[32,512]{1,0:T(8,128)S(1)}, f32[32,512]{1,0:T(8,128)S(1)}, u32[]{:S(2)}, u32[]{:S(2)}) collective-permute-start(f32[32,512]{1,0:T(8,128)S(1)} %slice_select_fusion.18), channel_id=1, source_target_pairs={{0,16},{1,17},{2,18},{3,19},{4,20},{5,21},{6,22},{7,23},{8,24},{9,... | collective-permute-start | bytes 196616 | tf_op jit(solution)/shard_map/ppermute | solution.py:590
  268.1 5.3 %collective-permute-start.48 = (f32[32,512]{1,0:T(8,128)S(1)}, f32[32,512]{1,0:T(8,128)S(1)}, u32[]{:S(2)}, u32[]{:S(2)}) collective-permute-start(f32[32,512]{1,0:T(8,128)S(1)} %select_add_fusion.17), channel_id=1, source_target_pairs={{0,16},{1,17},{2,18},{3,19},{4,20},{5,21},{6,22},{7,23},{8,24},{9,... | collective-permute-start | bytes 196616 | tf_op jit(solution)/shard_map/ppermute | solution.py:590
  270.0 5.5 %collective-permute-start.40 = (f32[32,512]{1,0:T(8,128)S(1)}, f32[32,512]{1,0:T(8,128)S(1)}, u32[]{:S(2)}, u32[]{:S(2)}) collective-permute-start(f32[32,512]{1,0:T(8,128)S(1)} %select_add_fusion.18), channel_id=1, source_target_pairs={{0,16},{1,17},{2,18},{3,19},{4,20},{5,21},{6,22},{7,23},{8,24},{9,... | collective-permute-start | bytes 196616 | tf_op jit(solution)/shard_map/ppermute | solution.py:590
  273.4 5.0 %collective-permute-start.49 = (f32[64,512]{1,0:T(8,128)S(1)}, f32[64,512]{1,0:T(8,128)S(1)}, u32[]{:S(2)}, u32[]{:S(2)}) collective-permute-start(f32[64,512]{1,0:T(8,128)S(1)} %pad_maximum_fusion.20), channel_id=1, source_target_pairs={{0,8},{1,9},{2,10},{3,11},{4,12},{5,13},{6,14},{7,15},{8,0},{9,1},... | collective-permute-start | bytes 393224 | tf_op jit(solution)/shard_map/ppermute | solution.py:590
  275.6 5.0 %collective-permute-start.41 = (f32[64,512]{1,0:T(8,128)S(1)}, f32[64,512]{1,0:T(8,128)S(1)}, u32[]{:S(2)}, u32[]{:S(2)}) collective-permute-start(f32[64,512]{1,0:T(8,128)S(1)} %pad_maximum_fusion.19), channel_id=1, source_target_pairs={{0,8},{1,9},{2,10},{3,11},{4,12},{5,13},{6,14},{7,15},{8,0},{9,1},... | collective-permute-start | bytes 393224 | tf_op jit(solution)/shard_map/ppermute | solution.py:590
  278.5 6.4 %collective-permute-start.50 = (f32[128,512]{1,0:T(8,128)S(1)}, f32[128,512]{1,0:T(8,128)S(1)}, u32[]{:S(2)}, u32[]{:S(2)}) collective-permute-start(f32[128,512]{1,0:T(8,128)S(1)} %pad_maximum_fusion.14), channel_id=1, source_target_pairs={{0,2},{1,3},{2,0},{3,1},{4,6},{5,7},{6,4},{7,5},{8,10},{9,11},{10,... | collective-permute-start | bytes 786440 | tf_op jit(solution)/shard_map/ppermute | solution.py:590
  280.7 6.4 %collective-permute-start.42 = (f32[128,512]{1,0:T(8,128)S(1)}, f32[128,512]{1,0:T(8,128)S(1)}, u32[]{:S(2)}, u32[]{:S(2)}) collective-permute-start(f32[128,512]{1,0:T(8,128)S(1)} %pad_maximum_fusion.13), channel_id=1, source_target_pairs={{0,4},{1,5},{2,6},{3,7},{4,0},{5,1},{6,2},{7,3},{8,12},{9,13},{10,... | collective-permute-start | bytes 786440 | tf_op jit(solution)/shard_map/ppermute | solution.py:590
  285.1 9.2 %collective-permute-start.51 = (f32[256,512]{1,0:T(8,128)S(1)}, f32[256,512]{1,0:T(8,128)S(1)}, u32[]{:S(2)}, u32[]{:S(2)}) collective-permute-start(f32[256,512]{1,0:T(8,128)S(1)} %pad_maximum_fusion.10), channel_id=1, source_target_pairs={{0,4},{1,5},{2,6},{3,7},{4,0},{5,1},{6,2},{7,3},{8,12},{9,13},{10,... | collective-permute-start | bytes 1572872 | tf_op jit(solution)/shard_map/ppermute | solution.py:590
  287.2 9.2 %collective-permute-start.43 = (f32[256,512]{1,0:T(8,128)S(1)}, f32[256,512]{1,0:T(8,128)S(1)}, u32[]{:S(2)}, u32[]{:S(2)}) collective-permute-start(f32[256,512]{1,0:T(8,128)S(1)} %pad_maximum_fusion.9), channel_id=1, source_target_pairs={{0,2},{1,3},{2,0},{3,1},{4,6},{5,7},{6,4},{7,5},{8,10},{9,11},{10,... | collective-permute-start | bytes 1572872 | tf_op jit(solution)/shard_map/ppermute | solution.py:590
  289.8 20.3 %collective-permute-start.70 = (f32[768,512]{1,0:T(8,128)}, f32[768,512]{1,0:T(8,128)}, u32[]{:S(2)}, u32[]{:S(2)}) collective-permute-start(f32[768,512]{1,0:T(8,128)} %pad_maximum_fusion.1), channel_id=1, source_target_pairs={{0,1},{1,0},{2,3},{3,2},{4,5},{5,4},{6,7},{7,6},{8,9},{9,8},{10,11... | collective-permute-start | bytes 4718600 | tf_op jit(solution)/shard_map/ppermute | solution.py:590
  298.0 14.1 %collective-permute-start.52 = (f32[1024,512]{1,0:T(8,128)}, f32[1024,512]{1,0:T(8,128)}, u32[]{:S(2)}, u32[]{:S(2)}) collective-permute-start(f32[1024,512]{1,0:T(8,128)} %pad_maximum_fusion), channel_id=1, source_target_pairs={{0,1},{1,0},{2,3},{3,2},{4,5},{5,4},{6,7},{7,6},{8,9},{9,8},{10,11... | collective-permute-start | bytes 6291464 | tf_op jit(solution)/shard_map/ppermute | solution.py:590
  299.5 9.2 %collective-permute-start.34 = (f32[256,512]{1,0:T(8,128)}, f32[256,512]{1,0:T(8,128)}, u32[]{:S(2)}, u32[]{:S(2)}) collective-permute-start(f32[256,512]{1,0:T(8,128)} %pad_maximum_fusion.8), channel_id=1, source_target_pairs={{0,1},{1,0},{2,3},{3,2},{4,5},{5,4},{6,7},{7,6},{8,9},{9,8},{10,11... | collective-permute-start | bytes 1572872 | tf_op jit(solution)/shard_map/ppermute | solution.py:590
  (31 other events, 259.5 us)
